TPU v7x, 768 devices: a whole 4x8x12 slice. The times are simulated.
768 devices in a mesh: face: 96 (over z, y), tile: 8 (over x, core).
Axes of the slice: x: 4, y: 8, z: 12, core: 2. Of those that a mesh axis runs over, the one named last changes fastest.
Arguments:
- climate_state: float32 [8, 768, 1024], P(None, 'face', 'tile'), may hold values from -6 to 6
- diffusive_courant: float32 [768, 1024], P('face', 'tile'), may hold values from 0.02 to 0.24
- stratum_projection: float32 [8, 8], replicated, may hold values from -2 to 2
- destination_piece: int32 [67584], P(('face', 'tile')), may hold values from 0 to 703, as said below
- shared_footprints: bfloat16 [67584, 128, 128], P(('face', 'tile')), may hold values from 0.019897461 to 0.19921875
- oceanic_departure: float32 [67584, 128], P(('face', 'tile')), may hold values from -6 to 6
- wet_indicator: int32 [67584, 128], P(('face', 'tile')), may hold values 0 or 1
- heating_response: float32 [8], replicated, may hold values from -1 to 1
Outputs:
- stepped_weather_fields: float32 [8, 768, 1024], P(None, 'face', 'tile')
- stepped_seawater_kelvin: float32 [67584, 128], P(('face', 'tile'))
- regridded_seawater_kelvin: float32 [768, 1024], P('face', 'tile')
Inputs may be any that keep to these rules, and one draw needn't show every extreme that they name: destination_piece[p] // 88 is the tile index of the ocean block's owner within the pair's face group and destination_piece[p] % 88 the block on it. Within a face group every ocean block is named by exactly one pair. The 88 pairs of one device name at most 22 blocks of one tile index, and every device names exactly 22 of some tile index.
All inputs are finite; a program needn't handle non-finite values. No bound on the sum of `wet_indicator` on one device may be relied on, other than what follows from the above.
Results may differ from a plain program's by a relative error of at most 0.0018.
Values may be sent and summed in bfloat16 or wider, within the bound.
A program may use at most 32 MiB of HBM per device.

v0:
```python
import jax
import jax.numpy as jnp
from jax import lax
from jax.sharding import PartitionSpec as P

SUBSTEPS = 6


def padded_2(array, sides, width):
    for axis, dim in sides:
        count, length = (lax.axis_size(axis), array.shape[dim])
        up = [(i, (i + 1) % count) for i in range(count)]
        down = [(j, i) for i, j in up]
        last = lax.slice_in_dim(array, length - width, length, axis=dim)
        leading = lax.slice_in_dim(array, 0, width, axis=dim)
        before = lax.ppermute(last, axis, up)
        after = lax.ppermute(leading, axis, down)
        array = jnp.concatenate([before, array, after], axis=dim)
    return array


def stencil(padded, coeff):
    inner = padded[:, 1:-1, 1:-1]
    beside_all = (
        padded[:, 2:, 1:-1] + padded[:, :-2, 1:-1] + padded[:, 1:-1, 2:] + padded[:, 1:-1, :-2]
    )
    return inner + coeff * (beside_all - 4.0 * inner)


def surface(stratum_projection, stepped_weather_fields):
    return jnp.tanh(
        jnp.einsum(
            "fl,lxy->fxy",
            stratum_projection,
            stepped_weather_fields,
            precision=lax.Precision.HIGHEST,
        )
    )


def body(
    climate_state,
    diffusive_courant,
    stratum_projection,
    destination_piece,
    shared_footprints,
    oceanic_departure,
    wet_indicator,
    heating_response,
):
    vertical_levels, coupled_pair_ledger, lattice_nodes = climate_state.shape
    nflux = stratum_projection.shape[0]
    flux = jnp.zeros((nflux, coupled_pair_ledger, lattice_nodes), jnp.float32)
    stepped_weather_fields = climate_state
    for step in range(SUBSTEPS):
        padded = padded_2(stepped_weather_fields, (("face", 1), ("tile", 2)), 1)
        stepped_weather_fields = stencil(padded, diffusive_courant)
        flux = flux + surface(stratum_projection, stepped_weather_fields)
    flux_low = (flux * (1.0 / SUBSTEPS)).astype(jnp.bfloat16)
    pairs = destination_piece.shape[0]
    neighbour_fanout = pairs // coupled_pair_ledger
    processor_piece_sequence = oceanic_departure.shape[0]
    tiles = lax.axis_size("tile")
    slots = 2 * pairs // tiles
    ones_cells = jnp.ones((lattice_nodes,), jnp.bfloat16)
    colsum = jnp.einsum(
        "pac,a->pc", shared_footprints, ones_cells, preferred_element_type=jnp.float32
    )
    horizontal_totalled = jnp.einsum(
        "pac,c->pa", shared_footprints, ones_cells, preferred_element_type=jnp.float32
    )
    source_cells = jnp.repeat(jnp.transpose(flux_low, (1, 0, 2)), neighbour_fanout, axis=0)
    unremapped_flux = jnp.einsum(
        "rkd,rdy->rky", source_cells, shared_footprints, preferred_element_type=jnp.float32
    )
    partial_value = (unremapped_flux * (1.0 / colsum)[:, None, :]).astype(jnp.bfloat16)
    owner = destination_piece // processor_piece_sequence
    local = destination_piece % processor_piece_sequence
    own_hot = (owner[:, None] == jnp.arange(tiles, dtype=jnp.int32)[None, :]).astype(jnp.int32)
    rank = jnp.sum((jnp.cumsum(own_hot, 0) - own_hot) * own_hot, 1)
    position = owner * slots + rank
    placed = position[:, None] == jnp.arange(tiles * slots, dtype=jnp.int32)[None, :]
    outbound = jnp.einsum(
        "ps,pk->sk",
        placed.astype(jnp.bfloat16),
        partial_value.reshape(pairs, nflux * lattice_nodes),
        preferred_element_type=jnp.float32,
    ).astype(jnp.bfloat16)
    target = jnp.sum(jnp.where(placed, local[:, None], 0), 0) + jnp.where(
        jnp.any(placed, 0), 0, processor_piece_sequence
    )
    inbound, arrived = (
        lax.all_to_all(outbound, "tile", split_axis=0, concat_axis=0, tiled=True),
        lax.all_to_all(target, "tile", split_axis=0, concat_axis=0, tiled=True),
    )
    block_is_active = (
        arrived[None, :] == jnp.arange(processor_piece_sequence, dtype=jnp.int32)[:, None]
    ).astype(jnp.bfloat16)
    fluxes = jnp.dot(block_is_active, inbound, preferred_element_type=jnp.float32).reshape(
        processor_piece_sequence, nflux, lattice_nodes
    )
    bottom_driving_terms = jnp.einsum(
        "f,ofc->oc", heating_response, fluxes, precision=lax.Precision.HIGHEST
    )
    stepped_seawater_kelvin = (
        oceanic_departure + wet_indicator.astype(jnp.float32) * bottom_driving_terms
    )
    back = jnp.einsum(
        "qz,qu->zu",
        block_is_active.astype(jnp.float32),
        stepped_seawater_kelvin,
        precision=lax.Precision.HIGHEST,
    )
    returned = lax.all_to_all(back, "tile", split_axis=0, concat_axis=0, tiled=True)
    coupling_coefficients = jnp.dot(
        placed.astype(jnp.float32), returned, precision=lax.Precision.HIGHEST
    )
    enthalpy_passage = jnp.einsum(
        "pac,pc->pa",
        shared_footprints.astype(jnp.float32),
        coupling_coefficients,
        precision=lax.Precision.HIGHEST,
    )
    regridded_seawater_kelvin = enthalpy_passage.reshape(
        coupled_pair_ledger, neighbour_fanout, lattice_nodes
    ).sum(1) / horizontal_totalled.reshape(
        coupled_pair_ledger, neighbour_fanout, lattice_nodes
    ).sum(
        1
    )
    return (stepped_weather_fields, stepped_seawater_kelvin, regridded_seawater_kelvin)


def solution(mesh):
    return jax.shard_map(
        body,
        mesh=mesh,
        in_specs=(
            P(None, "face", "tile"),
            P("face", "tile"),
            P(),
            P(("face", "tile")),
            P(("face", "tile"), None, None),
            P(("face", "tile"), None),
            P(("face", "tile"), None),
            P(),
        ),
        out_specs=(P(None, "face", "tile"), P(("face", "tile"), None), P("face", "tile")),
        check_vma=False,
    )
```

profile of v0, /device:TPU:1, one launch (start us, length us, event | category | flops | bytes accessed | tf_op | source)
XLA Modules:
  0.0 154.9 jit_solution(16217522125603314076)
XLA Ops:
  1.6 18.0 %collective-permute-start = (f32[8,1,128]{2,1,0:T(1,128)S(1)}, f32[8,1,128]{2,1,0:T(1,128)S(1)}, u32[]{:S(2)}, u32[]{:S(2)}) collective-permute-start(f32[8,1,128]{2,1,0:T(1,128)S(1)} %get-tuple-element.26), channel_id=1, source_target_pairs={{8,0},{16,8},{24,16},{32,24},{40,32},{48,40},{56,48},{64,56},{72,6... | collective-permute-start | bytes 12296 | tf_op jit(solution)/shard_map/ppermute | solution.py:17
  19.6 1.9 %collective-permute-start.1 = (f32[8,1,128]{2,1,0:T(1,128)S(1)}, f32[8,1,128]{2,1,0:T(1,128)S(1)}, u32[]{:S(2)}, u32[]{:S(2)}) collective-permute-start(f32[8,1,128]{2,1,0:T(1,128)S(1)} %get-tuple-element.25), channel_id=1, source_target_pairs={{0,8},{8,16},{16,24},{24,32},{32,40},{40,48},{48,56},{56,64},{64,7... | collective-permute-start | bytes 12296 | tf_op jit(solution)/shard_map/ppermute | solution.py:16
  22.6 4.7 %collective-permute-done.1 = f32[8,1,128]{2,1,0:T(1,128)S(1)} collective-permute-done((f32[8,1,128]{2,1,0:T(1,128)S(1)}, f32[8,1,128]{2,1,0:T(1,128)S(1)}, u32[]{:S(2)}, u32[]{:S(2)}) %collective-permute-start.1) | collective-permute-done | bytes 4128 | tf_op jit(solution)/shard_map/ppermute | solution.py:16
  28.2 2.1 %collective-permute-start.2 = (f32[8,10,1]{2,1,0:T(8,128)S(1)}, f32[8,10,1]{2,1,0:T(8,128)S(1)}, u32[]{:S(2)}, u32[]{:S(2)}) collective-permute-start(f32[8,10,1]{2,1,0:T(8,128)S(1)} %get-tuple-element.13), channel_id=1, source_target_pairs={{1,0},{2,1},{3,2},{4,3},{5,4},{6,5},{7,6},{0,7},{9,8},{10,9},{11,1... | collective-permute-start | bytes 968 | tf_op jit(solution)/shard_map/ppermute | solution.py:17
  30.3 1.1 collective-permute-start.3
  31.4 1.9 %collective-permute-done.2 = f32[8,10,1]{2,1,0:T(8,128)S(1)} collective-permute-done((f32[8,10,1]{2,1,0:T(8,128)S(1)}, f32[8,10,1]{2,1,0:T(8,128)S(1)}, u32[]{:S(2)}, u32[]{:S(2)}) %collective-permute-start.2) | collective-permute-done | bytes 352 | tf_op jit(solution)/shard_map/ppermute | solution.py:17
  34.4 1.9 %collective-permute-start.4 = (f32[8,1,128]{2,1,0:T(1,128)S(1)}, f32[8,1,128]{2,1,0:T(1,128)S(1)}, u32[]{:S(2)}, u32[]{:S(2)}) collective-permute-start(f32[8,1,128]{2,1,0:T(1,128)S(1)} %get-tuple-element.24), channel_id=1, source_target_pairs={{8,0},{16,8},{24,16},{32,24},{40,32},{48,40},{56,48},{64,56},{72,6... | collective-permute-start | bytes 12296 | tf_op jit(solution)/shard_map/ppermute | solution.py:17
  36.3 3.4 %collective-permute-start.5 = (f32[8,1,128]{2,1,0:T(1,128)S(1)}, f32[8,1,128]{2,1,0:T(1,128)S(1)}, u32[]{:S(2)}, u32[]{:S(2)}) collective-permute-start(f32[8,1,128]{2,1,0:T(1,128)S(1)} %get-tuple-element.23), channel_id=1, source_target_pairs={{0,8},{8,16},{16,24},{24,32},{32,40},{40,48},{48,56},{56,64},{64,7... | collective-permute-start | bytes 12296 | tf_op jit(solution)/shard_map/ppermute | solution.py:16
  39.8 4.2 %collective-permute-done.5 = f32[8,1,128]{2,1,0:T(1,128)S(1)} collective-permute-done((f32[8,1,128]{2,1,0:T(1,128)S(1)}, f32[8,1,128]{2,1,0:T(1,128)S(1)}, u32[]{:S(2)}, u32[]{:S(2)}) %collective-permute-start.5) | collective-permute-done | bytes 4128 | tf_op jit(solution)/shard_map/ppermute | solution.py:16
  44.1 4.2 %collective-permute-start.6 = (f32[8,10,1]{2,1,0:T(8,128)S(1)}, f32[8,10,1]{2,1,0:T(8,128)S(1)}, u32[]{:S(2)}, u32[]{:S(2)}) collective-permute-start(f32[8,10,1]{2,1,0:T(8,128)S(1)} %get-tuple-element.11), channel_id=1, source_target_pairs={{1,0},{2,1},{3,2},{4,3},{5,4},{6,5},{7,6},{0,7},{9,8},{10,9},{11,1... | collective-permute-start | bytes 968 | tf_op jit(solution)/shard_map/ppermute | solution.py:17
  50.4 1.9 %collective-permute-start.8 = (f32[8,1,128]{2,1,0:T(1,128)S(1)}, f32[8,1,128]{2,1,0:T(1,128)S(1)}, u32[]{:S(2)}, u32[]{:S(2)}) collective-permute-start(f32[8,1,128]{2,1,0:T(1,128)S(1)} %get-tuple-element.22), channel_id=1, source_target_pairs={{8,0},{16,8},{24,16},{32,24},{40,32},{48,40},{56,48},{64,56},{72,6... | collective-permute-start | bytes 12296 | tf_op jit(solution)/shard_map/ppermute | solution.py:17
  52.4 3.4 %collective-permute-start.9 = (f32[8,1,128]{2,1,0:T(1,128)S(1)}, f32[8,1,128]{2,1,0:T(1,128)S(1)}, u32[]{:S(2)}, u32[]{:S(2)}) collective-permute-start(f32[8,1,128]{2,1,0:T(1,128)S(1)} %get-tuple-element.21), channel_id=1, source_target_pairs={{0,8},{8,16},{16,24},{24,32},{32,40},{40,48},{48,56},{56,64},{64,7... | collective-permute-start | bytes 12296 | tf_op jit(solution)/shard_map/ppermute | solution.py:16
  56.4 7.4 %all-to-all-start = ((s32[8,22,1]{1,2,0:T(1,128)}), s32[8,22,1]{1,2,0:T(1,128)S(1)}, u32[]{:S(2)}, u32[]{:S(2)}) async-start(s32[8,22,1]{1,2,0:T(1,128)} %bitcast.1), calls=%async_computation | async-start | bytes 8192 | tf_op jit(solution)/shard_map/all_to_all | solution.py:94
  66.1 1.8 %collective-permute-done.10 = f32[8,10,1]{2,1,0:T(8,128)S(1)} collective-permute-done((f32[8,10,1]{2,1,0:T(8,128)S(1)}, f32[8,10,1]{2,1,0:T(8,128)S(1)}, u32[]{:S(2)}, u32[]{:S(2)}) %collective-permute-start.10) | collective-permute-done | bytes 352 | tf_op jit(solution)/shard_map/ppermute | solution.py:17
  68.0 5.0 %collective-permute-start.12 = (f32[8,1,128]{2,1,0:T(1,128)S(1)}, f32[8,1,128]{2,1,0:T(1,128)S(1)}, u32[]{:S(2)}, u32[]{:S(2)}) collective-permute-start(f32[8,1,128]{2,1,0:T(1,128)S(1)} %get-tuple-element.20), channel_id=1, source_target_pairs={{8,0},{16,8},{24,16},{32,24},{40,32},{48,40},{56,48},{64,56},{72,6... | collective-permute-start | bytes 12296 | tf_op jit(solution)/shard_map/ppermute | solution.py:17
  73.0 1.9 %collective-permute-start.13 = (f32[8,1,128]{2,1,0:T(1,128)S(1)}, f32[8,1,128]{2,1,0:T(1,128)S(1)}, u32[]{:S(2)}, u32[]{:S(2)}) collective-permute-start(f32[8,1,128]{2,1,0:T(1,128)S(1)} %get-tuple-element.19), channel_id=1, source_target_pairs={{0,8},{8,16},{16,24},{24,32},{32,40},{40,48},{48,56},{56,64},{64,7... | collective-permute-start | bytes 12296 | tf_op jit(solution)/shard_map/ppermute | solution.py:16
  74.9 5.7 %collective-permute-done.13 = f32[8,1,128]{2,1,0:T(1,128)S(1)} collective-permute-done((f32[8,1,128]{2,1,0:T(1,128)S(1)}, f32[8,1,128]{2,1,0:T(1,128)S(1)}, u32[]{:S(2)}, u32[]{:S(2)}) %collective-permute-start.13) | collective-permute-done | bytes 4128 | tf_op jit(solution)/shard_map/ppermute | solution.py:16
  80.8 5.4 %collective-permute-start.14 = (f32[8,10,1]{2,1,0:T(8,128)S(1)}, f32[8,10,1]{2,1,0:T(8,128)S(1)}, u32[]{:S(2)}, u32[]{:S(2)}) collective-permute-start(f32[8,10,1]{2,1,0:T(8,128)S(1)} %get-tuple-element.7), channel_id=1, source_target_pairs={{1,0},{2,1},{3,2},{4,3},{5,4},{6,5},{7,6},{0,7},{9,8},{10,9},{11,1... | collective-permute-start | bytes 968 | tf_op jit(solution)/shard_map/ppermute | solution.py:17
  87.6 1.9 %collective-permute-start.16 = (f32[8,1,128]{2,1,0:T(1,128)S(1)}, f32[8,1,128]{2,1,0:T(1,128)S(1)}, u32[]{:S(2)}, u32[]{:S(2)}) collective-permute-start(f32[8,1,128]{2,1,0:T(1,128)S(1)} %get-tuple-element.18), channel_id=1, source_target_pairs={{8,0},{16,8},{24,16},{32,24},{40,32},{48,40},{56,48},{64,56},{72,6... | collective-permute-start | bytes 12296 | tf_op jit(solution)/shard_map/ppermute | solution.py:17
  89.5 3.4 %collective-permute-start.17 = (f32[8,1,128]{2,1,0:T(1,128)S(1)}, f32[8,1,128]{2,1,0:T(1,128)S(1)}, u32[]{:S(2)}, u32[]{:S(2)}) collective-permute-start(f32[8,1,128]{2,1,0:T(1,128)S(1)} %get-tuple-element.17), channel_id=1, source_target_pairs={{0,8},{8,16},{16,24},{24,32},{32,40},{40,48},{48,56},{56,64},{64,7... | collective-permute-start | bytes 12296 | tf_op jit(solution)/shard_map/ppermute | solution.py:16
  93.1 4.1 %collective-permute-done.17 = f32[8,1,128]{2,1,0:T(1,128)S(1)} collective-permute-done((f32[8,1,128]{2,1,0:T(1,128)S(1)}, f32[8,1,128]{2,1,0:T(1,128)S(1)}, u32[]{:S(2)}, u32[]{:S(2)}) %collective-permute-start.17) | collective-permute-done | bytes 4128 | tf_op jit(solution)/shard_map/ppermute | solution.py:16
  97.3 4.7 %collective-permute-start.18 = (f32[8,10,1]{2,1,0:T(8,128)S(1)}, f32[8,10,1]{2,1,0:T(8,128)S(1)}, u32[]{:S(2)}, u32[]{:S(2)}) collective-permute-start(f32[8,10,1]{2,1,0:T(8,128)S(1)} %get-tuple-element.5), channel_id=1, source_target_pairs={{1,0},{2,1},{3,2},{4,3},{5,4},{6,5},{7,6},{0,7},{9,8},{10,9},{11,1... | collective-permute-start | bytes 968 | tf_op jit(solution)/shard_map/ppermute | solution.py:17
  103.5 1.9 %collective-permute-start.20 = (f32[8,1,128]{2,1,0:T(1,128)S(1)}, f32[8,1,128]{2,1,0:T(1,128)S(1)}, u32[]{:S(2)}, u32[]{:S(2)}) collective-permute-start(f32[8,1,128]{2,1,0:T(1,128)S(1)} %get-tuple-element.16), channel_id=1, source_target_pairs={{8,0},{16,8},{24,16},{32,24},{40,32},{48,40},{56,48},{64,56},{72,6... | collective-permute-start | bytes 12296 | tf_op jit(solution)/shard_map/ppermute | solution.py:17
  105.4 3.4 %collective-permute-start.21 = (f32[8,1,128]{2,1,0:T(1,128)S(1)}, f32[8,1,128]{2,1,0:T(1,128)S(1)}, u32[]{:S(2)}, u32[]{:S(2)}) collective-permute-start(f32[8,1,128]{2,1,0:T(1,128)S(1)} %get-tuple-element.15), channel_id=1, source_target_pairs={{0,8},{8,16},{16,24},{24,32},{32,40},{40,48},{48,56},{56,64},{64,7... | collective-permute-start | bytes 12296 | tf_op jit(solution)/shard_map/ppermute | solution.py:16
  109.0 4.1 %collective-permute-done.21 = f32[8,1,128]{2,1,0:T(1,128)S(1)} collective-permute-done((f32[8,1,128]{2,1,0:T(1,128)S(1)}, f32[8,1,128]{2,1,0:T(1,128)S(1)}, u32[]{:S(2)}, u32[]{:S(2)}) %collective-permute-start.21) | collective-permute-done | bytes 4128 | tf_op jit(solution)/shard_map/ppermute | solution.py:16
  113.2 4.7 %collective-permute-start.22 = (f32[8,10,1]{2,1,0:T(8,128)S(1)}, f32[8,10,1]{2,1,0:T(8,128)S(1)}, u32[]{:S(2)}, u32[]{:S(2)}) collective-permute-start(f32[8,10,1]{2,1,0:T(8,128)S(1)} %get-tuple-element.3), channel_id=1, source_target_pairs={{1,0},{2,1},{3,2},{4,3},{5,4},{6,5},{7,6},{0,7},{9,8},{10,9},{11,1... | collective-permute-start | bytes 968 | tf_op jit(solution)/shard_map/ppermute | solution.py:17
  121.7 6.9 %all-to-all-start.1 = ((bf16[8,22,1024]{2,1,0:T(8,128)(2,1)}), bf16[8,22,1024]{2,1,0:T(8,128)(2,1)S(1)}, u32[]{:S(2)}, u32[]{:S(2)}) async-start(bf16[8,22,1024]{2,1,0:T(8,128)(2,1)} %all_to_all.21), calls=%async_computation.1 | async-start | bytes 786432 | tf_op jit(solution)/shard_map/all_to_all | solution.py:93
  129.9 6.8 %all-to-all-done.1 = bf16[8,22,1024]{2,1,0:T(8,128)(2,1)S(1)} async-done(((bf16[8,22,1024]{2,1,0:T(8,128)(2,1)}), bf16[8,22,1024]{2,1,0:T(8,128)(2,1)S(1)}, u32[]{:S(2)}, u32[]{:S(2)}) %all-to-all-start.1) | async-done | bytes 360480 | tf_op jit(solution)/shard_map/all_to_all | solution.py:93
  137.6 1.2 fusion.9
  140.3 4.1 %all-to-all-start.2 = ((f32[8,22,128]{2,1,0:T(8,128)}), f32[8,22,128]{2,1,0:T(8,128)S(1)}, u32[]{:S(2)}, u32[]{:S(2)}) async-start(f32[8,22,128]{2,1,0:T(8,128)} %all_to_all.24), calls=%async_computation.2 | async-start | bytes 196608 | tf_op jit(solution)/shard_map/all_to_all | solution.py:114
  145.3 4.1 %all-to-all-done.2 = f32[8,22,128]{2,1,0:T(8,128)S(1)} async-done(((f32[8,22,128]{2,1,0:T(8,128)}), f32[8,22,128]{2,1,0:T(8,128)S(1)}, u32[]{:S(2)}, u32[]{:S(2)}) %all-to-all-start.2) | async-done | bytes 90144 | tf_op jit(solution)/shard_map/all_to_all | solution.py:114
  149.7 4.5 %fusion.92 = f32[88,1,128]{2,1,0:T(1,128)S(1)} fusion(f32[88,128,1]{1,2,0:T(1,128)S(1)} %bitcast.66, bf16[88,128,128]{2,1,0:T(8,128)(2,1)S(1)} %copy-done), kind=kOutput, calls=%fused_computation.165 | convolution fusion | flops 17301504 | bytes 2973696 | tf_op jit(solution)/shard_map/pac,pc->pa/dot_general | solution.py:118
  (99 shorter events, 21.9 us)
Async XLA Ops:
  0.6 65.0 %copy-start = (bf16[88,128,128]{2,1,0:T(8,128)(2,1)S(1)}, bf16[88,128,128]{2,1,0:T(8,128)(2,1)}, u32[]{:S(2)}) copy-start(bf16[88,128,128]{2,1,0:T(8,128)(2,1)} %param.12) | copy-start | bytes 8650756
  0.6 67.2 %copy-start.2 = (f32[8,128]{1,0:T(8,128)S(1)}, f32[8,128]{1,0:T(8,128)}, u32[]{:S(2)}) copy-start(f32[8,128]{1,0:T(8,128)} %param.9) | copy-start | bytes 12292
  0.7 85.5 %copy-start.3 = (f32[8,8]{1,0:T(8,128)S(1)}, f32[8,8]{1,0:T(8,128)}, u32[]{:S(2)}) copy-start(f32[8,8]{1,0:T(8,128)} %param.10) | copy-start | bytes 772
  1.6 21.0 %collective-permute-start = (f32[8,1,128]{2,1,0:T(1,128)S(1)}, f32[8,1,128]{2,1,0:T(1,128)S(1)}, u32[]{:S(2)}, u32[]{:S(2)}) collective-permute-start(f32[8,1,128]{2,1,0:T(1,128)S(1)} %get-tuple-element.26), channel_id=1, source_target_pairs={{8,0},{16,8},{24,16},{32,24},{40,32},{48,40},{56,48},{64,56},{72,6... | collective-permute-start | bytes 12296 | tf_op jit(solution)/shard_map/ppermute | solution.py:17
  19.6 7.7 %collective-permute-start.1 = (f32[8,1,128]{2,1,0:T(1,128)S(1)}, f32[8,1,128]{2,1,0:T(1,128)S(1)}, u32[]{:S(2)}, u32[]{:S(2)}) collective-permute-start(f32[8,1,128]{2,1,0:T(1,128)S(1)} %get-tuple-element.25), channel_id=1, source_target_pairs={{0,8},{8,16},{16,24},{24,32},{32,40},{40,48},{48,56},{56,64},{64,7... | collective-permute-start | bytes 12296 | tf_op jit(solution)/shard_map/ppermute | solution.py:16
  28.2 5.2 %collective-permute-start.2 = (f32[8,10,1]{2,1,0:T(8,128)S(1)}, f32[8,10,1]{2,1,0:T(8,128)S(1)}, u32[]{:S(2)}, u32[]{:S(2)}) collective-permute-start(f32[8,10,1]{2,1,0:T(8,128)S(1)} %get-tuple-element.13), channel_id=1, source_target_pairs={{1,0},{2,1},{3,2},{4,3},{5,4},{6,5},{7,6},{0,7},{9,8},{10,9},{11,1... | collective-permute-start | bytes 968 | tf_op jit(solution)/shard_map/ppermute | solution.py:17
  30.3 3.0 %collective-permute-start.3 = (f32[8,10,1]{2,1,0:T(8,128)S(1)}, f32[8,10,1]{2,1,0:T(8,128)S(1)}, u32[]{:S(2)}, u32[]{:S(2)}) collective-permute-start(f32[8,10,1]{2,1,0:T(8,128)S(1)} %get-tuple-element.14), channel_id=1, source_target_pairs={{0,1},{1,2},{2,3},{3,4},{4,5},{5,6},{6,7},{7,0},{8,9},{9,10},{10,1... | collective-permute-start | bytes 968 | tf_op jit(solution)/shard_map/ppermute | solution.py:16
  34.4 5.4 %collective-permute-start.4 = (f32[8,1,128]{2,1,0:T(1,128)S(1)}, f32[8,1,128]{2,1,0:T(1,128)S(1)}, u32[]{:S(2)}, u32[]{:S(2)}) collective-permute-start(f32[8,1,128]{2,1,0:T(1,128)S(1)} %get-tuple-element.24), channel_id=1, source_target_pairs={{8,0},{16,8},{24,16},{32,24},{40,32},{48,40},{56,48},{64,56},{72,6... | collective-permute-start | bytes 12296 | tf_op jit(solution)/shard_map/ppermute | solution.py:17
  36.3 7.7 %collective-permute-start.5 = (f32[8,1,128]{2,1,0:T(1,128)S(1)}, f32[8,1,128]{2,1,0:T(1,128)S(1)}, u32[]{:S(2)}, u32[]{:S(2)}) collective-permute-start(f32[8,1,128]{2,1,0:T(1,128)S(1)} %get-tuple-element.23), channel_id=1, source_target_pairs={{0,8},{8,16},{16,24},{24,32},{32,40},{40,48},{48,56},{56,64},{64,7... | collective-permute-start | bytes 12296 | tf_op jit(solution)/shard_map/ppermute | solution.py:16
  44.1 5.1 %collective-permute-start.6 = (f32[8,10,1]{2,1,0:T(8,128)S(1)}, f32[8,10,1]{2,1,0:T(8,128)S(1)}, u32[]{:S(2)}, u32[]{:S(2)}) collective-permute-start(f32[8,10,1]{2,1,0:T(8,128)S(1)} %get-tuple-element.11), channel_id=1, source_target_pairs={{1,0},{2,1},{3,2},{4,3},{5,4},{6,5},{7,6},{0,7},{9,8},{10,9},{11,1... | collective-permute-start | bytes 968 | tf_op jit(solution)/shard_map/ppermute | solution.py:17
  48.3 1.3 collective-permute-start.7
  50.4 13.3 %collective-permute-start.8 = (f32[8,1,128]{2,1,0:T(1,128)S(1)}, f32[8,1,128]{2,1,0:T(1,128)S(1)}, u32[]{:S(2)}, u32[]{:S(2)}) collective-permute-start(f32[8,1,128]{2,1,0:T(1,128)S(1)} %get-tuple-element.22), channel_id=1, source_target_pairs={{8,0},{16,8},{24,16},{32,24},{40,32},{48,40},{56,48},{64,56},{72,6... | collective-permute-start | bytes 12296 | tf_op jit(solution)/shard_map/ppermute | solution.py:17
  52.4 11.4 %collective-permute-start.9 = (f32[8,1,128]{2,1,0:T(1,128)S(1)}, f32[8,1,128]{2,1,0:T(1,128)S(1)}, u32[]{:S(2)}, u32[]{:S(2)}) collective-permute-start(f32[8,1,128]{2,1,0:T(1,128)S(1)} %get-tuple-element.21), channel_id=1, source_target_pairs={{0,8},{8,16},{16,24},{24,32},{32,40},{40,48},{48,56},{56,64},{64,7... | collective-permute-start | bytes 12296 | tf_op jit(solution)/shard_map/ppermute | solution.py:16
  56.4 65.3 %all-to-all-start = ((s32[8,22,1]{1,2,0:T(1,128)}), s32[8,22,1]{1,2,0:T(1,128)S(1)}, u32[]{:S(2)}, u32[]{:S(2)}) async-start(s32[8,22,1]{1,2,0:T(1,128)} %bitcast.1), calls=%async_computation | async-start | bytes 8192 | tf_op jit(solution)/shard_map/all_to_all | solution.py:94
  63.9 4.0 %collective-permute-start.10 = (f32[8,10,1]{2,1,0:T(8,128)S(1)}, f32[8,10,1]{2,1,0:T(8,128)S(1)}, u32[]{:S(2)}, u32[]{:S(2)}) collective-permute-start(f32[8,10,1]{2,1,0:T(8,128)S(1)} %get-tuple-element.9), channel_id=1, source_target_pairs={{1,0},{2,1},{3,2},{4,3},{5,4},{6,5},{7,6},{0,7},{9,8},{10,9},{11,1... | collective-permute-start | bytes 968 | tf_op jit(solution)/shard_map/ppermute | solution.py:17
  64.9 3.0 %collective-permute-start.11 = (f32[8,10,1]{2,1,0:T(8,128)S(1)}, f32[8,10,1]{2,1,0:T(8,128)S(1)}, u32[]{:S(2)}, u32[]{:S(2)}) collective-permute-start(f32[8,10,1]{2,1,0:T(8,128)S(1)} %get-tuple-element.10), channel_id=1, source_target_pairs={{0,1},{1,2},{2,3},{3,4},{4,5},{5,6},{6,7},{7,0},{8,9},{9,10},{10,1... | collective-permute-start | bytes 968 | tf_op jit(solution)/shard_map/ppermute | solution.py:16
  68.0 6.9 %collective-permute-start.12 = (f32[8,1,128]{2,1,0:T(1,128)S(1)}, f32[8,1,128]{2,1,0:T(1,128)S(1)}, u32[]{:S(2)}, u32[]{:S(2)}) collective-permute-start(f32[8,1,128]{2,1,0:T(1,128)S(1)} %get-tuple-element.20), channel_id=1, source_target_pairs={{8,0},{16,8},{24,16},{32,24},{40,32},{48,40},{56,48},{64,56},{72,6... | collective-permute-start | bytes 12296 | tf_op jit(solution)/shard_map/ppermute | solution.py:17
  73.0 7.7 %collective-permute-start.13 = (f32[8,1,128]{2,1,0:T(1,128)S(1)}, f32[8,1,128]{2,1,0:T(1,128)S(1)}, u32[]{:S(2)}, u32[]{:S(2)}) collective-permute-start(f32[8,1,128]{2,1,0:T(1,128)S(1)} %get-tuple-element.19), channel_id=1, source_target_pairs={{0,8},{8,16},{16,24},{24,32},{32,40},{40,48},{48,56},{56,64},{64,7... | collective-permute-start | bytes 12296 | tf_op jit(solution)/shard_map/ppermute | solution.py:16
  80.8 6.3 %collective-permute-start.14 = (f32[8,10,1]{2,1,0:T(8,128)S(1)}, f32[8,10,1]{2,1,0:T(8,128)S(1)}, u32[]{:S(2)}, u32[]{:S(2)}) collective-permute-start(f32[8,10,1]{2,1,0:T(8,128)S(1)} %get-tuple-element.7), channel_id=1, source_target_pairs={{1,0},{2,1},{3,2},{4,3},{5,4},{6,5},{7,6},{0,7},{9,8},{10,9},{11,1... | collective-permute-start | bytes 968 | tf_op jit(solution)/shard_map/ppermute | solution.py:17
  86.1 1.3 collective-permute-start.15
  87.6 5.5 %collective-permute-start.16 = (f32[8,1,128]{2,1,0:T(1,128)S(1)}, f32[8,1,128]{2,1,0:T(1,128)S(1)}, u32[]{:S(2)}, u32[]{:S(2)}) collective-permute-start(f32[8,1,128]{2,1,0:T(1,128)S(1)} %get-tuple-element.18), channel_id=1, source_target_pairs={{8,0},{16,8},{24,16},{32,24},{40,32},{48,40},{56,48},{64,56},{72,6... | collective-permute-start | bytes 12296 | tf_op jit(solution)/shard_map/ppermute | solution.py:17
  89.5 7.7 %collective-permute-start.17 = (f32[8,1,128]{2,1,0:T(1,128)S(1)}, f32[8,1,128]{2,1,0:T(1,128)S(1)}, u32[]{:S(2)}, u32[]{:S(2)}) collective-permute-start(f32[8,1,128]{2,1,0:T(1,128)S(1)} %get-tuple-element.17), channel_id=1, source_target_pairs={{0,8},{8,16},{16,24},{24,32},{32,40},{40,48},{48,56},{56,64},{64,7... | collective-permute-start | bytes 12296 | tf_op jit(solution)/shard_map/ppermute | solution.py:16
  97.3 5.6 %collective-permute-start.18 = (f32[8,10,1]{2,1,0:T(8,128)S(1)}, f32[8,10,1]{2,1,0:T(8,128)S(1)}, u32[]{:S(2)}, u32[]{:S(2)}) collective-permute-start(f32[8,10,1]{2,1,0:T(8,128)S(1)} %get-tuple-element.5), channel_id=1, source_target_pairs={{1,0},{2,1},{3,2},{4,3},{5,4},{6,5},{7,6},{0,7},{9,8},{10,9},{11,1... | collective-permute-start | bytes 968 | tf_op jit(solution)/shard_map/ppermute | solution.py:17
  102.0 1.3 collective-permute-start.19
  103.5 5.5 %collective-permute-start.20 = (f32[8,1,128]{2,1,0:T(1,128)S(1)}, f32[8,1,128]{2,1,0:T(1,128)S(1)}, u32[]{:S(2)}, u32[]{:S(2)}) collective-permute-start(f32[8,1,128]{2,1,0:T(1,128)S(1)} %get-tuple-element.16), channel_id=1, source_target_pairs={{8,0},{16,8},{24,16},{32,24},{40,32},{48,40},{56,48},{64,56},{72,6... | collective-permute-start | bytes 12296 | tf_op jit(solution)/shard_map/ppermute | solution.py:17
  105.4 7.7 %collective-permute-start.21 = (f32[8,1,128]{2,1,0:T(1,128)S(1)}, f32[8,1,128]{2,1,0:T(1,128)S(1)}, u32[]{:S(2)}, u32[]{:S(2)}) collective-permute-start(f32[8,1,128]{2,1,0:T(1,128)S(1)} %get-tuple-element.15), channel_id=1, source_target_pairs={{0,8},{8,16},{16,24},{24,32},{32,40},{40,48},{48,56},{56,64},{64,7... | collective-permute-start | bytes 12296 | tf_op jit(solution)/shard_map/ppermute | solution.py:16
  113.2 5.6 %collective-permute-start.22 = (f32[8,10,1]{2,1,0:T(8,128)S(1)}, f32[8,10,1]{2,1,0:T(8,128)S(1)}, u32[]{:S(2)}, u32[]{:S(2)}) collective-permute-start(f32[8,10,1]{2,1,0:T(8,128)S(1)} %get-tuple-element.3), channel_id=1, source_target_pairs={{1,0},{2,1},{3,2},{4,3},{5,4},{6,5},{7,6},{0,7},{9,8},{10,9},{11,1... | collective-permute-start | bytes 968 | tf_op jit(solution)/shard_map/ppermute | solution.py:17
  117.9 1.3 collective-permute-start.23
  119.6 19.7 %copy-start.5 = (f32[88,128]{1,0:T(8,128)S(1)}, f32[88,128]{1,0:T(8,128)}, u32[]{:S(2)}) copy-start(f32[88,128]{1,0:T(8,128)} %param.13) | copy-start | bytes 135172
  119.6 19.7 %copy-start.6 = (s32[88,128]{1,0:T(8,128)S(1)}, s32[88,128]{1,0:T(8,128)}, u32[]{:S(2)}) copy-start(s32[88,128]{1,0:T(8,128)} %param.14) | copy-start | bytes 135172
  121.7 15.0 %all-to-all-start.1 = ((bf16[8,22,1024]{2,1,0:T(8,128)(2,1)}), bf16[8,22,1024]{2,1,0:T(8,128)(2,1)S(1)}, u32[]{:S(2)}, u32[]{:S(2)}) async-start(bf16[8,22,1024]{2,1,0:T(8,128)(2,1)} %all_to_all.21), calls=%async_computation.1 | async-start | bytes 786432 | tf_op jit(solution)/shard_map/all_to_all | solution.py:93
  140.3 9.1 %all-to-all-start.2 = ((f32[8,22,128]{2,1,0:T(8,128)}), f32[8,22,128]{2,1,0:T(8,128)S(1)}, u32[]{:S(2)}, u32[]{:S(2)}) async-start(f32[8,22,128]{2,1,0:T(8,128)} %all_to_all.24), calls=%async_computation.2 | async-start | bytes 196608 | tf_op jit(solution)/shard_map/all_to_all | solution.py:114
  (3 other events, 52.3 us)
where the time goes:
time: 156 us; the launch traced here: 155 us
  starting transfers between devices  90.4 us (58%)
  waiting for transfers between devices  42.2 us (27%)
  matrix products  10.3 us (7%)
  other arithmetic  5.72 us (4%)
  local copies, waits for them, and re-layouts  5.18 us (3%)
    ppermute x12, starting transfers between devices, padded_2(): after = lax.ppermute(leading, axis, down)  52.8 us
    ppermute x12, waiting for transfers between devices, padded_2(): before = lax.ppermute(last, axis, up)  24.5 us
    ppermute x12, starting transfers between devices, padded_2(): before = lax.ppermute(last, axis, up)  19.2 us
    all_to_all x1, starting transfers between devices, body(): lax.all_to_all(target, 'tile', split_axis=0, concat_axis=0, tiled=True)  7.35 us
    all_to_all x1, starting transfers between devices, body(): lax.all_to_all(outbound, 'tile', split_axis=0, concat_axis=0, tiled=True)  6.93 us
    all_to_all x1, waiting for transfers between devices, body(): lax.all_to_all(outbound, 'tile', split_axis=0, concat_axis=0, tiled=True)  6.84 us
    ppermute x12, waiting for transfers between devices, padded_2(): after = lax.ppermute(leading, axis, down)  6.67 us
    dot_general x1, matrix products, body(): jnp.einsum('pac,pc->pa', shared_footprints.astype(jnp.float32), coupling_...  4.55 us
  transfers between devices with their start and end apart: 27, of which 17 were waited for; matrix products, arithmetic and copies ran while one was open for 5% of the time, Pallas kernels for 0%

commit v1 on v0

v1 whole, which is shorter than its diff:
```python
import functools

import jax
import jax.numpy as jnp
from jax import lax
from jax.experimental import pallas as pl
from jax.experimental.pallas import tpu as pltpu
from jax.sharding import PartitionSpec as P

MESH = pl.DeviceIdType.MESH
F32 = jnp.float32
BF16 = jnp.bfloat16
SUBSTEPS = 6
LEV = 8
ROWS = 8
CELLS = 128
PAIRS = 88
FAN = 11
BLOCKS = 88
TILES = 8
SLOTS = 24


def halves(x):
    hi = x.astype(BF16)
    return hi, (x - hi.astype(F32)).astype(BF16)


def select_rows(onehot, x):
    hi, lo = halves(x)
    both = jnp.dot(onehot, jnp.concatenate([hi, lo], 1), preferred_element_type=F32)
    return both[:, :CELLS] + both[:, CELLS:]


def kernel(
    faces,
    state_hbm, courant_hbm, proj_hbm, dest_hbm, w_hbm, dep_hbm, wet_hbm, heat_hbm,
    state_out, sea_out, regrid_out,
    state_v, courant_v, proj_v, dest_all, w_v, dep_v, wet_v, heat_s,
    pack, strip_first, strip_last, rows_above, rows_below, side,
    recip, den, hsum, place_t, onehot, onehot_t, place,
    sea_send, sea_recv, h_send, h_recv,
    local_sem, halo_send_sem, halo_recv_sem, peer_send_sem, peer_recv_sem,
):
    f = lax.axis_index("face")
    t = lax.axis_index("tile")
    up, down = lax.rem(f + faces - 1, faces), lax.rem(f + 1, faces)
    left, right = lax.rem(t + TILES - 1, TILES), lax.rem(t + 1, TILES)

    loads = [
        pltpu.make_async_copy(src, dst, local_sem.at[i])
        for i, (src, dst) in enumerate([
            (state_hbm, state_v), (courant_hbm, courant_v), (dest_hbm, dest_all.at[t]), (proj_hbm, proj_v),
            (heat_hbm, heat_s), (w_hbm, w_v), (dep_hbm, dep_v), (wet_hbm, wet_v),
        ])
    ]
    for load in loads:
        load.start()

    barrier = pltpu.get_barrier_semaphore()
    greet = [(fa, ti) for fa in (up, down) for ti in (left, t, right)]
    greet += [(f, lax.rem(t + k, TILES)) for k in range(1, TILES)]
    for device in greet:
        pl.semaphore_signal(barrier, inc=1, device_id=device, device_id_type=MESH)

    for k in range(3):
        side[k, 8:120, :] = jnp.zeros((112, CELLS), F32)
    for i in range(5):
        loads[i].wait()
    courant = courant_v[...]
    pack[0:8, :] = courant
    pack[72:80, :] = courant
    for r in range(ROWS):
        pack[8 + 8 * r:16 + 8 * r, :] = state_v[pl.ds(r, LEV, stride=ROWS), :]
    own = jnp.concatenate([pack[0:72, :], jnp.zeros((56, CELLS), F32)], 0)
    own_t = jnp.swapaxes(own, 0, 1)
    strip_first[...] = own_t[0:8]
    strip_last[...] = own_t[120:128]

    pl.semaphore_wait(barrier, len(greet))

    dest_copies, halo_copies = [], []
    for k in range(1, TILES):
        dest_copies.append(pltpu.make_async_remote_copy(
            src_ref=dest_all.at[t], dst_ref=dest_all.at[t], send_sem=peer_send_sem.at[k - 1], recv_sem=peer_recv_sem.at[k - 1],
            device_id=(f, lax.rem(t + k, TILES)), device_id_type=MESH))
    halo = [
        (pack.at[pl.ds(0, 56)], rows_below, (up, t)),
        (pack.at[pl.ds(24, 56)], rows_above, (down, t)),
    ]
    for face, slot in ((up, 2), (f, 1), (down, 0)):
        halo.append((strip_first, side.at[slot, pl.ds(0, 8)], (face, left)))
        halo.append((strip_last, side.at[slot, pl.ds(120, 8)], (face, right)))
    for i, (src, dst, device) in enumerate(halo):
        halo_copies.append(pltpu.make_async_remote_copy(
            src_ref=src, dst_ref=dst, send_sem=halo_send_sem.at[i], recv_sem=halo_recv_sem.at[i],
            device_id=device, device_id_type=MESH))
    for copy in dest_copies + halo_copies:
        copy.start()

    i0 = lax.broadcasted_iota(jnp.int32, (PAIRS, PAIRS), 0)
    i1 = lax.broadcasted_iota(jnp.int32, (PAIRS, PAIRS), 1)
    earlier = (i0 < i1).astype(F32).astype(BF16)
    div8 = sum((i1 >= 8 * m).astype(jnp.int32) for m in range(1, FAN))
    permute = (i0 == (i1 - 8 * div8) * FAN + div8).astype(F32).astype(BF16)
    slot_id = lax.broadcasted_iota(jnp.int32, (SLOTS, PAIRS), 0).astype(F32)
    tile_id = lax.broadcasted_iota(jnp.int32, (TILES, PAIRS), 0)

    def owner_of(dest):
        return sum((dest >= BLOCKS * m).astype(jnp.int32) for m in range(1, TILES))

    def slots_of(mask):
        wide = jnp.concatenate([mask, jnp.zeros((8, PAIRS), F32)], 0).astype(BF16)
        rank = jnp.dot(wide, earlier, preferred_element_type=F32)[:8]
        rank = jnp.where(mask > 0.5, rank, -1.0)
        return jnp.concatenate(
            [(rank[i:i + 1] == slot_id).astype(F32) for i in range(TILES)], 0)

    mine = jnp.broadcast_to(owner_of(dest_all[t]), (TILES, PAIRS))
    own_place = slots_of((mine == tile_id).astype(F32))
    placed = jnp.dot(own_place.astype(BF16), permute, preferred_element_type=F32)
    place[...] = placed.astype(BF16)
    placed = jnp.concatenate([placed, jnp.zeros((TILES * SLOTS, CELLS - PAIRS), F32)], 1)
    place_t[...] = jnp.swapaxes(placed, 0, 1)[:PAIRS].astype(BF16)

    for copy in dest_copies:
        copy.wait()
    dest = jnp.concatenate([dest_all[i] for i in range(TILES)], 0)
    owner = owner_of(dest)
    local = (dest - BLOCKS * owner + 1).astype(F32)
    asked = slots_of((owner == t).astype(F32))
    block = jnp.concatenate([
        jnp.sum(asked[SLOTS * i:SLOTS * (i + 1)] * local[i:i + 1], axis=1, keepdims=True) for i in range(TILES)], 0)
    block_id = (lax.broadcasted_iota(jnp.int32, (TILES * SLOTS, CELLS), 1) + 1).astype(F32)
    hot = (jnp.broadcast_to(block, (TILES * SLOTS, CELLS)) == block_id).astype(F32)
    onehot_t[...] = jnp.swapaxes(hot, 0, 1)[:BLOCKS].astype(BF16)
    hot = hot[:, :BLOCKS].astype(BF16)
    loads[6].wait()
    loads[7].wait()
    hi, lo = halves(dep_v[...])
    wet = wet_v[...].astype(F32)
    found = jnp.dot(hot, jnp.concatenate([hi, lo, wet.astype(BF16)], 1), preferred_element_type=F32)
    found_dep = found[:, :CELLS] + found[:, CELLS:2 * CELLS]
    found_wet = found[:, 2 * CELLS:]
    for i in range(TILES):
        sea_send[i, 0:SLOTS, :] = found_dep[SLOTS * i:SLOTS * (i + 1)]
        sea_send[i, SLOTS:2 * SLOTS, :] = found_wet[SLOTS * i:SLOTS * (i + 1)]
    sea_copies = []
    for k in range(1, TILES):
        peer = lax.rem(t + k, TILES)
        sea_copies.append(pltpu.make_async_remote_copy(
            src_ref=sea_send.at[peer], dst_ref=sea_recv.at[t],
            send_sem=peer_send_sem.at[6 + k], recv_sem=peer_recv_sem.at[6 + k],
            device_id=(f, peer), device_id_type=MESH))
        sea_copies[-1].start()
    sea_recv[t] = sea_send[t]

    loads[5].wait()
    sums = []
    for r in range(ROWS):
        total = jnp.zeros((CELLS, CELLS), F32)
        for j in range(FAN):
            w = w_v[r * FAN + j].astype(F32)
            total = total + w
            recip[8 * j + r:8 * j + r + 1, :] = jnp.sum(w, axis=0, keepdims=True)
        sums.append(jnp.sum(jnp.swapaxes(total, 0, 1), axis=0, keepdims=True))
    den[...] = jnp.concatenate(sums, 0)
    recip[...] = 1.0 / recip[...]

    proj = proj_v[...]
    levels = [jnp.broadcast_to(proj[:, l:l + 1], (LEV, CELLS)) for l in range(LEV)]
    sub = lax.broadcasted_iota(jnp.int32, (8, CELLS), 0)
    heat = jnp.zeros((8, CELLS), F32)
    for i in range(8):
        heat = jnp.where(sub == i, heat_s[i], heat)
    lane = lax.broadcasted_iota(jnp.int32, (8, CELLS), 1)
    first, last = lane == 0, lane == CELLS - 1

    for copy in halo_copies:
        copy.wait()
    sides = [jnp.swapaxes(side[k], 0, 1) for k in range(3)]
    main = [rows_above[8 * i:8 * i + 8, :] for i in range(6)]
    main += [pack[8 + 8 * r:16 + 8 * r, :] for r in range(ROWS)]
    main += [rows_below[8 + 8 * i:16 + 8 * i, :] for i in range(6)]
    outer = [sides[0][8 + 8 * r:16 + 8 * r] for r in range(2, 8)]
    outer += [sides[1][8 + 8 * r:16 + 8 * r] for r in range(8)]
    outer += [sides[2][8 + 8 * r:16 + 8 * r] for r in range(6)]
    cm = [rows_above[48 + r:49 + r, :] for r in range(2, 8)]
    cm += [courant_v[r:r + 1, :] for r in range(8)]
    cm += [rows_below[r:r + 1, :] for r in range(6)]
    co = [sides[0][r:r + 1] for r in range(2, 8)]
    co += [sides[1][r:r + 1] for r in range(8)]
    co += [sides[2][r:r + 1] for r in range(6)]

    flux = [jnp.zeros((8, CELLS), F32) for _ in range(ROWS)]
    for step in range(SUBSTEPS):
        new_main, new_outer = list(main), list(outer)
        for j in range(step + 1, 19 - step):
            m, o = main[j], outer[j]
            m_next, o_next = pltpu.roll(m, CELLS - 1, 1), pltpu.roll(o, CELLS - 1, 1)
            m_prev, o_prev = pltpu.roll(m, 1, 1), pltpu.roll(o, 1, 1)
            around = main[j + 1] + main[j - 1] + jnp.where(last, o_next, m_next) + jnp.where(first, o_prev, m_prev)
            new_main[j] = m + cm[j] * (around - 4.0 * m)
            if step < SUBSTEPS - 1:
                around = outer[j + 1] + outer[j - 1] + jnp.where(last, m_next, o_next) + jnp.where(first, m_prev, o_prev)
                new_outer[j] = o + co[j] * (around - 4.0 * o)
        main, outer = new_main, new_outer
        for r in range(ROWS):
            x = main[6 + r]
            total = levels[0] * x[0:1]
            for l in range(1, LEV):
                total = total + levels[l] * x[l:l + 1]
            flux[r] = flux[r] + jnp.tanh(total)
    for r in range(ROWS):
        state_out[pl.ds(r, LEV, stride=ROWS), :] = main[6 + r]

    weighted = []
    for r in range(ROWS):
        low = (flux[r] * (1.0 / SUBSTEPS)).astype(BF16).astype(F32)
        weighted.append(jnp.sum(low * heat, axis=0, keepdims=True))
    weighted = jnp.concatenate(weighted + [jnp.zeros((CELLS - 8, CELLS), F32)], 0)
    weighted = jnp.swapaxes(weighted, 0, 1)
    for r in range(ROWS):
        column = jnp.broadcast_to(weighted[:, r:r + 1], (CELLS, CELLS))
        for j in range(FAN):
            hsum[8 * j + r:8 * j + r + 1, :] = jnp.sum(w_v[r * FAN + j].astype(F32) * column, axis=0, keepdims=True)
    drive = hsum[...] * recip[...]
    slots = select_rows(place[...], drive)
    for i in range(TILES):
        h_send[i] = slots[SLOTS * i:SLOTS * (i + 1)]
    h_copies = []
    for k in range(1, TILES):
        peer = lax.rem(t + k, TILES)
        h_copies.append(pltpu.make_async_remote_copy(
            src_ref=h_send.at[peer], dst_ref=h_recv.at[t],
            send_sem=peer_send_sem.at[13 + k], recv_sem=peer_recv_sem.at[13 + k],
            device_id=(f, peer), device_id_type=MESH))
        h_copies[-1].start()
    h_recv[t] = h_send[t]

    for copy in sea_copies:
        copy.wait()
    got_dep = jnp.concatenate([sea_recv[i, 0:SLOTS, :] for i in range(TILES)], 0)
    got_wet = jnp.concatenate([sea_recv[i, SLOTS:2 * SLOTS, :] for i in range(TILES)], 0)
    hi, lo = halves(got_dep)
    got = jnp.dot(place_t[...], jnp.concatenate([hi, lo, got_wet.astype(BF16)], 1), preferred_element_type=F32)
    hsum[...] = got[:, :CELLS] + got[:, CELLS:2 * CELLS] + got[:, 2 * CELLS:] * drive
    sums = []
    for r in range(ROWS):
        total = jnp.zeros((CELLS, CELLS), F32)
        for j in range(FAN):
            total = total + w_v[r * FAN + j].astype(F32) * hsum[8 * j + r:8 * j + r + 1, :]
        sums.append(jnp.sum(jnp.swapaxes(total, 0, 1), axis=0, keepdims=True))
    regrid_out[...] = jnp.concatenate(sums, 0) / den[...]

    for copy in h_copies:
        copy.wait()
    got = jnp.concatenate([h_recv[i] for i in range(TILES)], 0)
    sea_out[...] = dep_v[...] + wet_v[...].astype(F32) * select_rows(onehot_t[...], got)


def body(state, courant, proj, dest, w, dep, wet, heat):
    faces = lax.axis_size("face")
    vmem = pltpu.VMEM
    hbm = pl.BlockSpec(memory_space=pltpu.HBM)
    state, sea, regrid = pl.pallas_call(
        functools.partial(kernel, faces),
        out_shape=(
            jax.ShapeDtypeStruct((LEV * ROWS, CELLS), F32),
            jax.ShapeDtypeStruct((BLOCKS, CELLS), F32),
            jax.ShapeDtypeStruct((ROWS, CELLS), F32),
        ),
        in_specs=[hbm] * 8,
        out_specs=(pl.BlockSpec(memory_space=vmem),) * 3,
        scratch_shapes=[
            vmem((LEV * ROWS, CELLS), F32), vmem((ROWS, CELLS), F32), vmem((8, 8), F32),
            vmem((TILES, 1, PAIRS), jnp.int32), vmem((PAIRS, CELLS, CELLS), BF16),
            vmem((BLOCKS, CELLS), F32), vmem((BLOCKS, CELLS), jnp.int32), pltpu.SMEM((8,), F32),
            vmem((80, CELLS), F32), vmem((8, CELLS), F32), vmem((8, CELLS), F32),
            vmem((56, CELLS), F32), vmem((56, CELLS), F32), vmem((3, CELLS, CELLS), F32),
            vmem((PAIRS, CELLS), F32), vmem((ROWS, CELLS), F32), vmem((PAIRS, CELLS), F32),
            vmem((PAIRS, TILES * SLOTS), BF16), vmem((TILES * SLOTS, BLOCKS), BF16),
            vmem((BLOCKS, TILES * SLOTS), BF16), vmem((TILES * SLOTS, PAIRS), BF16),
            vmem((TILES, 2 * SLOTS, CELLS), F32), vmem((TILES, 2 * SLOTS, CELLS), F32),
            vmem((TILES, SLOTS, CELLS), F32), vmem((TILES, SLOTS, CELLS), F32),
            pltpu.SemaphoreType.DMA((8,)), pltpu.SemaphoreType.DMA((8,)), pltpu.SemaphoreType.DMA((8,)),
            pltpu.SemaphoreType.DMA((21,)), pltpu.SemaphoreType.DMA((21,)),
        ],
        compiler_params=pltpu.CompilerParams(
            collective_id=0, has_side_effects=True, vmem_limit_bytes=32 * 1024 * 1024),
    )(state.reshape(LEV * ROWS, CELLS), courant, proj, dest.reshape(1, PAIRS), w, dep, wet, heat)
    return state.reshape(LEV, ROWS, CELLS), sea, regrid


def solution(mesh):
    both = P(("face", "tile"), None)
    return jax.shard_map(
        body,
        mesh=mesh,
        in_specs=(
            P(None, "face", "tile"), P("face", "tile"), P(), P(("face", "tile")),
            P(("face", "tile"), None, None), both, both, P(),
        ),
        out_specs=(P(None, "face", "tile"), both, P("face", "tile")),
        check_vma=False,
    )
```

time: 156 us -> 40 us (0.26)
  starting transfers between devices: 90.4 us -> 0 us
  waiting for transfers between devices: 42.2 us -> 0 us
  Pallas kernels: 0 us -> 30.2 us
  matrix products: 10.3 us -> 0 us
  other arithmetic: 5.72 us -> 0 us
  local copies, waits for them, and re-layouts: 5.18 us -> 8.65 us
    ppermute x24 -> x0, starting transfers between devices: 72 us -> none  [the longest x12 52.8 us: padded_2(): after = lax.ppermute(leading, axis, down)]
    ppermute x24 -> x0, waiting for transfers between devices: 31.2 us -> none  [the longest x12 24.5 us: padded_2(): before = lax.ppermute(last, axis, up)]
    pallas_call x0 -> x1, Pallas kernels: none -> 30.2 us  [body(): pl.pallas_call(functools.partial(kernel, faces), out_shape=(jax.ShapeDtyp...]
    all_to_all x3 -> x0, starting transfers between devices: 18.4 us -> none  [the longest x1 7.35 us: body(): lax.all_to_all(target, 'tile', split_axis=0, concat_axis=0, tiled=True)]
    all_to_all x3 -> x0, waiting for transfers between devices: 11 us -> none  [the longest x1 6.84 us: body(): lax.all_to_all(outbound, 'tile', split_axis=0, concat_axis=0, tiled=True)]
    dot_general x15 -> x0, matrix products: 10.3 us -> none  [the longest x1 4.55 us: body(): jnp.einsum('pac,pc->pa', shared_footprints.astype(jnp.float32), coupling_...]
    unnamed x16 -> x19, local copies, waits for them, and re-layouts: 0.05 us -> 8.65 us
    all_to_all x5 -> x0, local copies, waits for them, and re-layouts: 2.88 us -> none  [the longest x2 1.7 us: body(): lax.all_to_all(outbound, 'tile', split_axis=0, concat_axis=0, tiled=True)]
  transfers between devices with their start and end apart: 27 -> 0, of which waited for: 17 -> 0; matrix products, arithmetic and copies ran while one was open for 5% -> 0% of each run, Pallas kernels for 0% -> 0%
where the time goes in v1:
time: 40 us; the launch traced here: 39.5 us
  Pallas kernels  30.2 us (76%)
  local copies, waits for them, and re-layouts  8.65 us (22%)
  between operations  0.66 us (2%)
    pallas_call x1, Pallas kernels, body(): pl.pallas_call(functools.partial(kernel, faces), out_shape=(jax.ShapeDtyp...  30.2 us
    unnamed x19, local copies, waits for them, and re-layouts  8.65 us

profile of v1, /device:TPU:1, one launch (start us, length us, event | category | flops | bytes accessed | tf_op | source)
XLA Modules:
  0.0 39.5 jit_solution(13222037365124514148)
XLA Ops:
  0.6 0.0 copy-start
  0.6 1.8 %copy-done = bf16[88,128,128]{2,1,0:T(8,128)(2,1)S(1)} copy-done((bf16[88,128,128]{2,1,0:T(8,128)(2,1)S(1)}, bf16[88,128,128]{2,1,0:T(8,128)(2,1)}, u32[]{:S(2)}) %copy-start) | copy-done | bytes 2883608
  2.4 0.0 copy-start.1
  2.5 0.8 %copy-done.1 = f32[88,128]{1,0:T(8,128)S(1)} copy-done((f32[88,128]{1,0:T(8,128)S(1)}, f32[88,128]{1,0:T(8,128)}, u32[]{:S(2)}) %copy-start.1) | copy-done | bytes 45080
  3.2 0.0 copy-start.2
  3.2 0.8 %copy-done.2 = s32[88,128]{1,0:T(8,128)S(1)} copy-done((s32[88,128]{1,0:T(8,128)S(1)}, s32[88,128]{1,0:T(8,128)}, u32[]{:S(2)}) %copy-start.2) | copy-done | bytes 45080
  4.0 0.0 copy-start.3
  4.0 0.8 %copy-done.3 = f32[8,8,128]{2,1,0:T(8,128)S(1)} copy-done((f32[8,8,128]{2,1,0:T(8,128)S(1)}, f32[8,8,128]{2,1,0:T(8,128)}, u32[]{:S(2)}) %copy-start.3) | copy-done | bytes 32792
  4.8 0.0 copy-start.4
  4.8 0.7 %copy-done.4 = f32[8,128]{1,0:T(8,128)S(1)} copy-done((f32[8,128]{1,0:T(8,128)S(1)}, f32[8,128]{1,0:T(8,128)}, u32[]{:S(2)}) %copy-start.4) | copy-done | bytes 4120
  5.5 0.0 copy-start.5
  5.5 0.7 %copy-done.5 = f32[8,8]{1,0:T(8,128)S(1)} copy-done((f32[8,8]{1,0:T(8,128)S(1)}, f32[8,8]{1,0:T(8,128)}, u32[]{:S(2)}) %copy-start.5) | copy-done | bytes 280
  6.2 0.0 copy-start.6
  6.2 0.7 %copy-done.6 = s32[88]{0:T(128)S(1)} copy-done((s32[88]{0:T(128)S(1)}, s32[88]{0:T(128)}, u32[]{:S(2)}) %copy-start.6) | copy-done | bytes 376
  6.8 0.0 copy-start.7
  6.8 0.7 %copy-done.7 = f32[8]{0:T(128)S(1)} copy-done((f32[8]{0:T(128)S(1)}, f32[8]{0:T(128)}, u32[]{:S(2)}) %copy-start.7) | copy-done | bytes 56
  7.5 30.2 %shard_map.103 = (f32[64,128]{1,0:T(8,128)S(1)}, f32[88,128]{1,0:T(8,128)S(1)}, f32[8,128]{1,0:T(8,128)S(1)}) custom-call(f32[64,128]{1,0:T(8,128)S(1)} %bitcast.3, f32[8,128]{1,0:T(8,128)S(1)} %copy-done.4, f32[8,8]{1,0:T(8,128)S(1)} %copy-done.5, s32[1,88]{1,0:T(1,128)S(1)} %bitcast.5, bf16[88,128,128]{2,1,0:T(8,128)(2,1)S(1)} %copy-done, ...), custom_call_target="tpu_custom_call" | custom-call | tf_op jit(solution)/shard_map/pallas_call | solution.py:266
  37.7 0.6 %copy.14 = f32[8,8,128]{2,1,0:T(8,128)} copy(f32[8,8,128]{2,1,0:T(8,128)S(1)} %bitcast.4) | data formatting | bytes 65536
  38.3 0.6 %copy.15 = f32[88,128]{1,0:T(8,128)} copy(f32[88,128]{1,0:T(8,128)S(1)} %get-tuple-element.13) | data formatting | bytes 90112
  39.0 0.6 %copy.16 = f32[8,128]{1,0:T(8,128)} copy(f32[8,128]{1,0:T(8,128)S(1)} %get-tuple-element.14) | data formatting | bytes 8192
Async XLA Ops:
  0.6 1.8 %copy-start = (bf16[88,128,128]{2,1,0:T(8,128)(2,1)S(1)}, bf16[88,128,128]{2,1,0:T(8,128)(2,1)}, u32[]{:S(2)}) copy-start(bf16[88,128,128]{2,1,0:T(8,128)(2,1)} %w_hbm.1) | copy-start | bytes 8650756
  2.4 0.8 %copy-start.1 = (f32[88,128]{1,0:T(8,128)S(1)}, f32[88,128]{1,0:T(8,128)}, u32[]{:S(2)}) copy-start(f32[88,128]{1,0:T(8,128)} %dep_hbm.1) | copy-start | bytes 135172
  3.2 0.8 %copy-start.2 = (s32[88,128]{1,0:T(8,128)S(1)}, s32[88,128]{1,0:T(8,128)}, u32[]{:S(2)}) copy-start(s32[88,128]{1,0:T(8,128)} %wet_hbm.1) | copy-start | bytes 135172
  4.0 0.8 %copy-start.3 = (f32[8,8,128]{2,1,0:T(8,128)S(1)}, f32[8,8,128]{2,1,0:T(8,128)}, u32[]{:S(2)}) copy-start(f32[8,8,128]{2,1,0:T(8,128)} %param.8) | copy-start | bytes 98308
  4.8 0.7 %copy-start.4 = (f32[8,128]{1,0:T(8,128)S(1)}, f32[8,128]{1,0:T(8,128)}, u32[]{:S(2)}) copy-start(f32[8,128]{1,0:T(8,128)} %courant_hbm.1) | copy-start | bytes 12292
  5.5 0.7 %copy-start.5 = (f32[8,8]{1,0:T(8,128)S(1)}, f32[8,8]{1,0:T(8,128)}, u32[]{:S(2)}) copy-start(f32[8,8]{1,0:T(8,128)} %proj_hbm.1) | copy-start | bytes 772
  6.2 0.7 %copy-start.6 = (s32[88]{0:T(128)S(1)}, s32[88]{0:T(128)}, u32[]{:S(2)}) copy-start(s32[88]{0:T(128)} %param.11) | copy-start | bytes 1060
  6.8 0.7 %copy-start.7 = (f32[8]{0:T(128)S(1)}, f32[8]{0:T(128)}, u32[]{:S(2)}) copy-start(f32[8]{0:T(128)} %heat_hbm.1) | copy-start | bytes 100

commit v2 on v1

--- a/solution.py
+++ b/solution.py
@@ -19,6 +19,8 @@
 BLOCKS = 88
 TILES = 8
 SLOTS = 24
+HOT_ROWS = 96
+VMEM_BYTES = 62 * 1024 * 1024
 
 
 def halves(x):
@@ -35,17 +37,23 @@
 def kernel(
     faces,
     state_hbm, courant_hbm, proj_hbm, dest_hbm, w_hbm, dep_hbm, wet_hbm, heat_hbm,
-    state_out, sea_out, regrid_out,
+    state_out, regrid_out, hot_out, h_recv,
     state_v, courant_v, proj_v, dest_all, w_v, dep_v, wet_v, heat_s,
     pack, strip_first, strip_last, rows_above, rows_below, side,
-    recip, den, hsum, place_t, onehot, onehot_t, place,
-    sea_send, sea_recv, h_send, h_recv,
+    recip, den, hsum, place_t, onehot_t, place, stepped, regrid,
+    sea_send, sea_recv, h_send,
     local_sem, halo_send_sem, halo_recv_sem, peer_send_sem, peer_recv_sem,
 ):
     f = lax.axis_index("face")
     t = lax.axis_index("tile")
     up, down = lax.rem(f + faces - 1, faces), lax.rem(f + 1, faces)
     left, right = lax.rem(t + TILES - 1, TILES), lax.rem(t + 1, TILES)
+
+    barrier = pltpu.get_barrier_semaphore()
+    greet = [(f, lax.rem(t + k, TILES)) for k in range(1, TILES)]
+    greet += [(fa, ti) for fa in (up, down) for ti in (left, t, right)]
+    for device in greet:
+        pl.semaphore_signal(barrier, inc=1, device_id=device, device_id_type=MESH)
 
     loads = [
         pltpu.make_async_copy(src, dst, local_sem.at[i])
@@ -54,19 +62,23 @@
             (heat_hbm, heat_s), (w_hbm, w_v), (dep_hbm, dep_v), (wet_hbm, wet_v),
         ])
     ]
-    for load in loads:
-        load.start()
-
-    barrier = pltpu.get_barrier_semaphore()
-    greet = [(fa, ti) for fa in (up, down) for ti in (left, t, right)]
-    greet += [(f, lax.rem(t + k, TILES)) for k in range(1, TILES)]
-    for device in greet:
-        pl.semaphore_signal(barrier, inc=1, device_id=device, device_id_type=MESH)
+    for i in (2, 0, 1, 3, 4):
+        loads[i].start()
 
     for k in range(3):
         side[k, 8:120, :] = jnp.zeros((112, CELLS), F32)
-    for i in range(5):
-        loads[i].wait()
+    pl.semaphore_wait(barrier, len(greet))
+    loads[2].wait()
+    dest_copies, halo_copies = [], []
+    for k in range(1, TILES):
+        dest_copies.append(pltpu.make_async_remote_copy(
+            src_ref=dest_all.at[t], dst_ref=dest_all.at[t], send_sem=peer_send_sem.at[k - 1], recv_sem=peer_recv_sem.at[k - 1],
+            device_id=(f, lax.rem(t + k, TILES)), device_id_type=MESH))
+    for copy in dest_copies:
+        copy.start()
+
+    loads[0].wait()
+    loads[1].wait()
     courant = courant_v[...]
     pack[0:8, :] = courant
     pack[72:80, :] = courant
@@ -77,13 +89,7 @@
     strip_first[...] = own_t[0:8]
     strip_last[...] = own_t[120:128]
 
-    pl.semaphore_wait(barrier, len(greet))
-
-    dest_copies, halo_copies = [], []
-    for k in range(1, TILES):
-        dest_copies.append(pltpu.make_async_remote_copy(
-            src_ref=dest_all.at[t], dst_ref=dest_all.at[t], send_sem=peer_send_sem.at[k - 1], recv_sem=peer_recv_sem.at[k - 1],
-            device_id=(f, lax.rem(t + k, TILES)), device_id_type=MESH))
+
     halo = [
         (pack.at[pl.ds(0, 56)], rows_below, (up, t)),
         (pack.at[pl.ds(24, 56)], rows_above, (down, t)),
@@ -95,8 +101,12 @@
         halo_copies.append(pltpu.make_async_remote_copy(
             src_ref=src, dst_ref=dst, send_sem=halo_send_sem.at[i], recv_sem=halo_recv_sem.at[i],
             device_id=device, device_id_type=MESH))
-    for copy in dest_copies + halo_copies:
+    for copy in halo_copies:
         copy.start()
+    for load in loads[5:]:
+        load.start()
+    loads[3].wait()
+    loads[4].wait()
 
     i0 = lax.broadcasted_iota(jnp.int32, (PAIRS, PAIRS), 0)
     i1 = lax.broadcasted_iota(jnp.int32, (PAIRS, PAIRS), 1)
@@ -122,6 +132,18 @@
     place[...] = placed.astype(BF16)
     placed = jnp.concatenate([placed, jnp.zeros((TILES * SLOTS, CELLS - PAIRS), F32)], 1)
     place_t[...] = jnp.swapaxes(placed, 0, 1)[:PAIRS].astype(BF16)
+
+    loads[5].wait()
+    sums = []
+    for r in range(ROWS):
+        total = jnp.zeros((CELLS, CELLS), F32)
+        for j in range(FAN):
+            w = w_v[r * FAN + j].astype(F32)
+            total = total + w
+            recip[8 * j + r:8 * j + r + 1, :] = jnp.sum(w, axis=0, keepdims=True)
+        sums.append(jnp.sum(jnp.swapaxes(total, 0, 1), axis=0, keepdims=True))
+    den[...] = jnp.concatenate(sums, 0)
+    recip[...] = 1.0 / recip[...]
 
     for copy in dest_copies:
         copy.wait()
@@ -133,7 +155,9 @@
         jnp.sum(asked[SLOTS * i:SLOTS * (i + 1)] * local[i:i + 1], axis=1, keepdims=True) for i in range(TILES)], 0)
     block_id = (lax.broadcasted_iota(jnp.int32, (TILES * SLOTS, CELLS), 1) + 1).astype(F32)
     hot = (jnp.broadcast_to(block, (TILES * SLOTS, CELLS)) == block_id).astype(F32)
-    onehot_t[...] = jnp.swapaxes(hot, 0, 1)[:BLOCKS].astype(BF16)
+    onehot_t[...] = jnp.swapaxes(hot, 0, 1)[:HOT_ROWS].astype(BF16)
+    outs = [pltpu.make_async_copy(onehot_t, hot_out, local_sem.at[9])]
+    outs[0].start()
     hot = hot[:, :BLOCKS].astype(BF16)
     loads[6].wait()
     loads[7].wait()
@@ -155,18 +179,6 @@
         sea_copies[-1].start()
     sea_recv[t] = sea_send[t]
 
-    loads[5].wait()
-    sums = []
-    for r in range(ROWS):
-        total = jnp.zeros((CELLS, CELLS), F32)
-        for j in range(FAN):
-            w = w_v[r * FAN + j].astype(F32)
-            total = total + w
-            recip[8 * j + r:8 * j + r + 1, :] = jnp.sum(w, axis=0, keepdims=True)
-        sums.append(jnp.sum(jnp.swapaxes(total, 0, 1), axis=0, keepdims=True))
-    den[...] = jnp.concatenate(sums, 0)
-    recip[...] = 1.0 / recip[...]
-
     proj = proj_v[...]
     levels = [jnp.broadcast_to(proj[:, l:l + 1], (LEV, CELLS)) for l in range(LEV)]
     sub = lax.broadcasted_iota(jnp.int32, (8, CELLS), 0)
@@ -212,7 +224,9 @@
                 total = total + levels[l] * x[l:l + 1]
             flux[r] = flux[r] + jnp.tanh(total)
     for r in range(ROWS):
-        state_out[pl.ds(r, LEV, stride=ROWS), :] = main[6 + r]
+        stepped[pl.ds(r, LEV, stride=ROWS), :] = main[6 + r]
+    outs.append(pltpu.make_async_copy(stepped, state_out, local_sem.at[8]))
+    outs[1].start()
 
     weighted = []
     for r in range(ROWS):
@@ -236,7 +250,8 @@
             send_sem=peer_send_sem.at[13 + k], recv_sem=peer_recv_sem.at[13 + k],
             device_id=(f, peer), device_id_type=MESH))
         h_copies[-1].start()
-    h_recv[t] = h_send[t]
+    outs.append(pltpu.make_async_copy(h_send.at[t], h_recv.at[t], local_sem.at[10]))
+    outs[2].start()
 
     for copy in sea_copies:
         copy.wait()
@@ -251,27 +266,56 @@
         for j in range(FAN):
             total = total + w_v[r * FAN + j].astype(F32) * hsum[8 * j + r:8 * j + r + 1, :]
         sums.append(jnp.sum(jnp.swapaxes(total, 0, 1), axis=0, keepdims=True))
-    regrid_out[...] = jnp.concatenate(sums, 0) / den[...]
-
-    for copy in h_copies:
+    regrid[...] = jnp.concatenate(sums, 0) / den[...]
+    outs.append(pltpu.make_async_copy(regrid, regrid_out, local_sem.at[11]))
+    outs[3].start()
+
+    for copy in outs + h_copies:
         copy.wait()
-    got = jnp.concatenate([h_recv[i] for i in range(TILES)], 0)
-    sea_out[...] = dep_v[...] + wet_v[...].astype(F32) * select_rows(onehot_t[...], got)
+
+
+def finish(
+    state_hbm, regrid_hbm, hot_hbm, drive_hbm, dep_hbm, wet_hbm,
+    state_out, sea_out, regrid_out,
+    state_v, regrid_v, hot_v, drive_v, dep_v, wet_v, sea_v, load_sem, store_sem,
+):
+    pairs = [(drive_hbm, drive_v), (hot_hbm, hot_v), (dep_hbm, dep_v), (wet_hbm, wet_v), (state_hbm, state_v), (regrid_hbm, regrid_v)]
+    loads = [pltpu.make_async_copy(src, dst, load_sem.at[i]) for i, (src, dst) in enumerate(pairs)]
+    for load in loads:
+        load.start()
+    stores = [
+        pltpu.make_async_copy(src, dst, store_sem.at[i])
+        for i, (src, dst) in enumerate([(state_v, state_out), (regrid_v, regrid_out), (sea_v, sea_out)])
+    ]
+    for load in loads[:4]:
+        load.wait()
+    drive = select_rows(hot_v[...], drive_v[...])[:BLOCKS]
+    sea_v[...] = dep_v[...] + wet_v[...].astype(F32) * drive
+    stores[2].start()
+    for i in range(2):
+        loads[4 + i].wait()
+        stores[i].start()
+    for store in stores:
+        store.wait()
 
 
 def body(state, courant, proj, dest, w, dep, wet, heat):
     faces = lax.axis_size("face")
     vmem = pltpu.VMEM
-    hbm = pl.BlockSpec(memory_space=pltpu.HBM)
-    state, sea, regrid = pl.pallas_call(
+    anywhere = pl.BlockSpec(memory_space=pl.ANY)
+    state_shape = jax.ShapeDtypeStruct((LEV * ROWS, CELLS), F32)
+    sea_shape = jax.ShapeDtypeStruct((BLOCKS, CELLS), F32)
+    regrid_shape = jax.ShapeDtypeStruct((ROWS, CELLS), F32)
+    state, regrid, hot, drive = pl.pallas_call(
         functools.partial(kernel, faces),
         out_shape=(
-            jax.ShapeDtypeStruct((LEV * ROWS, CELLS), F32),
-            jax.ShapeDtypeStruct((BLOCKS, CELLS), F32),
-            jax.ShapeDtypeStruct((ROWS, CELLS), F32),
+            state_shape,
+            regrid_shape,
+            jax.ShapeDtypeStruct((HOT_ROWS, TILES * SLOTS), BF16),
+            jax.ShapeDtypeStruct((TILES, SLOTS, CELLS), F32),
         ),
-        in_specs=[hbm] * 8,
-        out_specs=(pl.BlockSpec(memory_space=vmem),) * 3,
+        in_specs=[anywhere] * 8,
+        out_specs=(anywhere,) * 4,
         scratch_shapes=[
             vmem((LEV * ROWS, CELLS), F32), vmem((ROWS, CELLS), F32), vmem((8, 8), F32),
             vmem((TILES, 1, PAIRS), jnp.int32), vmem((PAIRS, CELLS, CELLS), BF16),
@@ -279,16 +323,26 @@
             vmem((80, CELLS), F32), vmem((8, CELLS), F32), vmem((8, CELLS), F32),
             vmem((56, CELLS), F32), vmem((56, CELLS), F32), vmem((3, CELLS, CELLS), F32),
             vmem((PAIRS, CELLS), F32), vmem((ROWS, CELLS), F32), vmem((PAIRS, CELLS), F32),
-            vmem((PAIRS, TILES * SLOTS), BF16), vmem((TILES * SLOTS, BLOCKS), BF16),
-            vmem((BLOCKS, TILES * SLOTS), BF16), vmem((TILES * SLOTS, PAIRS), BF16),
-            vmem((TILES, 2 * SLOTS, CELLS), F32), vmem((TILES, 2 * SLOTS, CELLS), F32),
-            vmem((TILES, SLOTS, CELLS), F32), vmem((TILES, SLOTS, CELLS), F32),
-            pltpu.SemaphoreType.DMA((8,)), pltpu.SemaphoreType.DMA((8,)), pltpu.SemaphoreType.DMA((8,)),
+            vmem((PAIRS, TILES * SLOTS), BF16), vmem((HOT_ROWS, TILES * SLOTS), BF16), vmem((TILES * SLOTS, PAIRS), BF16),
+            vmem((LEV * ROWS, CELLS), F32), vmem((ROWS, CELLS), F32),
+            vmem((TILES, 2 * SLOTS, CELLS), F32), vmem((TILES, 2 * SLOTS, CELLS), F32), vmem((TILES, SLOTS, CELLS), F32),
+            pltpu.SemaphoreType.DMA((12,)), pltpu.SemaphoreType.DMA((8,)), pltpu.SemaphoreType.DMA((8,)),
             pltpu.SemaphoreType.DMA((21,)), pltpu.SemaphoreType.DMA((21,)),
         ],
-        compiler_params=pltpu.CompilerParams(
-            collective_id=0, has_side_effects=True, vmem_limit_bytes=32 * 1024 * 1024),
+        compiler_params=pltpu.CompilerParams(collective_id=0, has_side_effects=True, vmem_limit_bytes=VMEM_BYTES),
     )(state.reshape(LEV * ROWS, CELLS), courant, proj, dest.reshape(1, PAIRS), w, dep, wet, heat)
+    state, sea, regrid = pl.pallas_call(
+        finish,
+        out_shape=(state_shape, sea_shape, regrid_shape),
+        in_specs=[anywhere] * 6,
+        out_specs=(anywhere,) * 3,
+        scratch_shapes=[
+            vmem((LEV * ROWS, CELLS), F32), vmem((ROWS, CELLS), F32), vmem((HOT_ROWS, TILES * SLOTS), BF16),
+            vmem((TILES * SLOTS, CELLS), F32), vmem((BLOCKS, CELLS), F32), vmem((BLOCKS, CELLS), jnp.int32),
+            vmem((BLOCKS, CELLS), F32), pltpu.SemaphoreType.DMA((6,)), pltpu.SemaphoreType.DMA((3,)),
+        ],
+        compiler_params=pltpu.CompilerParams(vmem_limit_bytes=VMEM_BYTES),
+    )(state, regrid, hot, drive.reshape(TILES * SLOTS, CELLS), dep, wet)
     return state.reshape(LEV, ROWS, CELLS), sea, regrid
 
 

time: 40 us -> 32.5 us (0.81)
  local copies, waits for them, and re-layouts: 8.65 us -> 0 us
  Pallas kernels: 30.2 us -> 31.6 us
    unnamed x19 -> x0, local copies, waits for them, and re-layouts: 8.65 us -> none
    pallas_call x1 -> x2, Pallas kernels: 30.2 us -> 31.6 us  [the longest x1 29.8 us: body(): pl.pallas_call(functools.partial(kernel, faces), out_shape=(state_shape,...]
where the time goes in v2:
time: 32.5 us; the launch traced here: 32.3 us
  Pallas kernels  31.6 us (97%)
  between operations  0.64 us (2%)
    pallas_call x1, Pallas kernels, body(): pl.pallas_call(functools.partial(kernel, faces), out_shape=(state_shape,...  29.8 us
    pallas_call x1, Pallas kernels, body(): pl.pallas_call(finish, out_shape=(state_shape, sea_shape, regrid_shape),...  1.77 us

profile of v2, /device:TPU:1, one launch (start us, length us, event | category | flops | bytes accessed | tf_op | source)
XLA Modules:
  0.0 32.3 jit_solution(7271779672548801628)
XLA Ops:
  0.6 29.8 %shard_map.103 = (f32[64,128]{1,0:T(8,128)}, f32[8,128]{1,0:T(8,128)}, bf16[96,192]{1,0:T(8,128)(2,1)}, f32[8,24,128]{2,1,0:T(8,128)}) custom-call(f32[64,128]{1,0:T(8,128)} %bitcast.5, f32[8,128]{1,0:T(8,128)} %courant_hbm.1, f32[8,8]{1,0:T(8,128)} %proj_hbm.1, s32[1,88]{1,0:T(1,128)} %bitcast.6, bf16[88,128,128]{2,1,0:T(8,128)(2,1)} %w_hbm.1, ...), custom_call_target="tpu_custom_call" | custom-call | tf_op jit(solution)/shard_map/pallas_call | solution.py:309
  30.5 1.8 %shard_map.104 = (f32[64,128]{1,0:T(8,128)}, f32[88,128]{1,0:T(8,128)}, f32[8,128]{1,0:T(8,128)}) custom-call(f32[64,128]{1,0:T(8,128)} %get-tuple-element.10.state_hbm, f32[8,128]{1,0:T(8,128)} %get-tuple-element.11.regrid_hbm, bf16[96,192]{1,0:T(8,128)(2,1)} %get-tuple-element.12.hot_hbm, f32[192,128]{1,0:T(8,128)} %bitcast.4, f32[88,128]{1,0:T(8,128)} %dep_hbm.3, ...), custom_call_target="tpu_custom_call" | custom-call | tf_op jit(solution)/shard_map/pallas_call | solution.py:334

commit v3 on v2

--- a/solution.py
+++ b/solution.py
@@ -19,6 +19,8 @@
 BLOCKS = 88
 TILES = 8
 SLOTS = 24
+SEA_ROWS = 80
+FAR_FIRST = (5, 3, 4, 2, 6, 7, 1)
 HOT_ROWS = 96
 VMEM_BYTES = 62 * 1024 * 1024
 
@@ -50,7 +52,7 @@
     left, right = lax.rem(t + TILES - 1, TILES), lax.rem(t + 1, TILES)
 
     barrier = pltpu.get_barrier_semaphore()
-    greet = [(f, lax.rem(t + k, TILES)) for k in range(1, TILES)]
+    greet = [(f, lax.rem(t + k, TILES)) for k in FAR_FIRST]
     greet += [(fa, ti) for fa in (up, down) for ti in (left, t, right)]
     for device in greet:
         pl.semaphore_signal(barrier, inc=1, device_id=device, device_id_type=MESH)
@@ -67,28 +69,28 @@
 
     for k in range(3):
         side[k, 8:120, :] = jnp.zeros((112, CELLS), F32)
+    loads[0].wait()
+    loads[1].wait()
+    courant = courant_v[...]
+    pack[0:8, :] = courant
+    pack[72:80, :] = courant
+    for r in range(ROWS):
+        pack[8 + 8 * r:16 + 8 * r, :] = state_v[pl.ds(r, LEV, stride=ROWS), :]
+    own = jnp.concatenate([pack[0:72, :], jnp.zeros((56, CELLS), F32)], 0)
+    own_t = jnp.swapaxes(own, 0, 1)
+    strip_first[...] = own_t[0:8]
+    strip_last[...] = own_t[120:128]
+
+
     pl.semaphore_wait(barrier, len(greet))
     loads[2].wait()
     dest_copies, halo_copies = [], []
-    for k in range(1, TILES):
+    for k in FAR_FIRST:
         dest_copies.append(pltpu.make_async_remote_copy(
             src_ref=dest_all.at[t], dst_ref=dest_all.at[t], send_sem=peer_send_sem.at[k - 1], recv_sem=peer_recv_sem.at[k - 1],
             device_id=(f, lax.rem(t + k, TILES)), device_id_type=MESH))
     for copy in dest_copies:
         copy.start()
-
-    loads[0].wait()
-    loads[1].wait()
-    courant = courant_v[...]
-    pack[0:8, :] = courant
-    pack[72:80, :] = courant
-    for r in range(ROWS):
-        pack[8 + 8 * r:16 + 8 * r, :] = state_v[pl.ds(r, LEV, stride=ROWS), :]
-    own = jnp.concatenate([pack[0:72, :], jnp.zeros((56, CELLS), F32)], 0)
-    own_t = jnp.swapaxes(own, 0, 1)
-    strip_first[...] = own_t[0:8]
-    strip_last[...] = own_t[120:128]
-
 
     halo = [
         (pack.at[pl.ds(0, 56)], rows_below, (up, t)),
@@ -145,32 +147,26 @@
     den[...] = jnp.concatenate(sums, 0)
     recip[...] = 1.0 / recip[...]
 
-    for copy in dest_copies:
-        copy.wait()
-    dest = jnp.concatenate([dest_all[i] for i in range(TILES)], 0)
-    owner = owner_of(dest)
-    local = (dest - BLOCKS * owner + 1).astype(F32)
-    asked = slots_of((owner == t).astype(F32))
-    block = jnp.concatenate([
-        jnp.sum(asked[SLOTS * i:SLOTS * (i + 1)] * local[i:i + 1], axis=1, keepdims=True) for i in range(TILES)], 0)
-    block_id = (lax.broadcasted_iota(jnp.int32, (TILES * SLOTS, CELLS), 1) + 1).astype(F32)
-    hot = (jnp.broadcast_to(block, (TILES * SLOTS, CELLS)) == block_id).astype(F32)
-    onehot_t[...] = jnp.swapaxes(hot, 0, 1)[:HOT_ROWS].astype(BF16)
-    outs = [pltpu.make_async_copy(onehot_t, hot_out, local_sem.at[9])]
-    outs[0].start()
-    hot = hot[:, :BLOCKS].astype(BF16)
     loads[6].wait()
     loads[7].wait()
     hi, lo = halves(dep_v[...])
-    wet = wet_v[...].astype(F32)
-    found = jnp.dot(hot, jnp.concatenate([hi, lo, wet.astype(BF16)], 1), preferred_element_type=F32)
-    found_dep = found[:, :CELLS] + found[:, CELLS:2 * CELLS]
-    found_wet = found[:, 2 * CELLS:]
+    blocks = jnp.concatenate([hi, lo, wet_v[...].astype(F32).astype(BF16)], 1)
+    block_id = (lax.broadcasted_iota(jnp.int32, (TILES * SLOTS, CELLS), 1) + 1).astype(F32)
+    for copy in dest_copies:
+        copy.wait()
+    local = jnp.concatenate([dest_all[i] for i in range(TILES)], 0) - BLOCKS * t
+    asked = slots_of(((local >= 0) & (local < BLOCKS)).astype(F32))
+    local = (local + 1).astype(F32)
+    block = jnp.concatenate([
+        jnp.sum(asked[SLOTS * i:SLOTS * (i + 1)] * local[i:i + 1], axis=1, keepdims=True) for i in range(TILES)], 0)
+    hot = (jnp.broadcast_to(block, (TILES * SLOTS, CELLS)) == block_id).astype(F32)
+    found = jnp.dot(hot[:, :BLOCKS].astype(BF16), blocks, preferred_element_type=F32)
     for i in range(TILES):
-        sea_send[i, 0:SLOTS, :] = found_dep[SLOTS * i:SLOTS * (i + 1)]
-        sea_send[i, SLOTS:2 * SLOTS, :] = found_wet[SLOTS * i:SLOTS * (i + 1)]
+        rows = found[SLOTS * i:SLOTS * (i + 1)]
+        rows = [rows[:, CELLS * part:CELLS * (part + 1)] for part in range(3)]
+        sea_send[i] = jnp.concatenate(rows + [jnp.zeros((SEA_ROWS - 3 * SLOTS, CELLS), F32)], 0).astype(BF16)
     sea_copies = []
-    for k in range(1, TILES):
+    for k in FAR_FIRST:
         peer = lax.rem(t + k, TILES)
         sea_copies.append(pltpu.make_async_remote_copy(
             src_ref=sea_send.at[peer], dst_ref=sea_recv.at[t],
@@ -178,6 +174,9 @@
             device_id=(f, peer), device_id_type=MESH))
         sea_copies[-1].start()
     sea_recv[t] = sea_send[t]
+    onehot_t[...] = jnp.swapaxes(hot, 0, 1)[:HOT_ROWS].astype(BF16)
+    outs = [pltpu.make_async_copy(onehot_t, hot_out, local_sem.at[9])]
+    outs[0].start()
 
     proj = proj_v[...]
     levels = [jnp.broadcast_to(proj[:, l:l + 1], (LEV, CELLS)) for l in range(LEV)]
@@ -243,7 +242,7 @@
     for i in range(TILES):
         h_send[i] = slots[SLOTS * i:SLOTS * (i + 1)]
     h_copies = []
-    for k in range(1, TILES):
+    for k in FAR_FIRST:
         peer = lax.rem(t + k, TILES)
         h_copies.append(pltpu.make_async_remote_copy(
             src_ref=h_send.at[peer], dst_ref=h_recv.at[t],
@@ -255,10 +254,9 @@
 
     for copy in sea_copies:
         copy.wait()
-    got_dep = jnp.concatenate([sea_recv[i, 0:SLOTS, :] for i in range(TILES)], 0)
-    got_wet = jnp.concatenate([sea_recv[i, SLOTS:2 * SLOTS, :] for i in range(TILES)], 0)
-    hi, lo = halves(got_dep)
-    got = jnp.dot(place_t[...], jnp.concatenate([hi, lo, got_wet.astype(BF16)], 1), preferred_element_type=F32)
+    pieces = [sea_recv[i].astype(F32) for i in range(TILES)]
+    parts = [jnp.concatenate([p[SLOTS * part:SLOTS * (part + 1)] for p in pieces], 0) for part in range(3)]
+    got = jnp.dot(place_t[...], jnp.concatenate(parts, 1).astype(BF16), preferred_element_type=F32)
     hsum[...] = got[:, :CELLS] + got[:, CELLS:2 * CELLS] + got[:, 2 * CELLS:] * drive
     sums = []
     for r in range(ROWS):
@@ -325,7 +323,7 @@
             vmem((PAIRS, CELLS), F32), vmem((ROWS, CELLS), F32), vmem((PAIRS, CELLS), F32),
             vmem((PAIRS, TILES * SLOTS), BF16), vmem((HOT_ROWS, TILES * SLOTS), BF16), vmem((TILES * SLOTS, PAIRS), BF16),
             vmem((LEV * ROWS, CELLS), F32), vmem((ROWS, CELLS), F32),
-            vmem((TILES, 2 * SLOTS, CELLS), F32), vmem((TILES, 2 * SLOTS, CELLS), F32), vmem((TILES, SLOTS, CELLS), F32),
+            vmem((TILES, SEA_ROWS, CELLS), BF16), vmem((TILES, SEA_ROWS, CELLS), BF16), vmem((TILES, SLOTS, CELLS), F32),
             pltpu.SemaphoreType.DMA((12,)), pltpu.SemaphoreType.DMA((8,)), pltpu.SemaphoreType.DMA((8,)),
             pltpu.SemaphoreType.DMA((21,)), pltpu.SemaphoreType.DMA((21,)),
         ],

time: 32.5 us -> 31.5 us (0.969)
  Pallas kernels: 31.6 us -> 30.5 us
    pallas_call x1, Pallas kernels: 29.8 us -> 28.8 us  [body(): pl.pallas_call(functools.partial(kernel, faces), out_shape=(state_shape,...]
where the time goes in v3:
time: 31.5 us; the launch traced here: 31.2 us
  Pallas kernels  30.5 us (97%)
  between operations  0.64 us (2%)
    pallas_call x1, Pallas kernels, body(): pl.pallas_call(functools.partial(kernel, faces), out_shape=(state_shape,...  28.8 us
    pallas_call x1, Pallas kernels, body(): pl.pallas_call(finish, out_shape=(state_shape, sea_shape, regrid_shape),...  1.77 us

profile of v3, /device:TPU:1, one launch (start us, length us, event | category | flops | bytes accessed | tf_op | source)
XLA Modules:
  0.0 31.2 jit_solution(8532271982772384872)
XLA Ops:
  0.6 28.8 %shard_map.103 = (f32[64,128]{1,0:T(8,128)}, f32[8,128]{1,0:T(8,128)}, bf16[96,192]{1,0:T(8,128)(2,1)}, f32[8,24,128]{2,1,0:T(8,128)}) custom-call(f32[64,128]{1,0:T(8,128)} %bitcast.5, f32[8,128]{1,0:T(8,128)} %courant_hbm.1, f32[8,8]{1,0:T(8,128)} %proj_hbm.1, s32[1,88]{1,0:T(1,128)} %bitcast.6, bf16[88,128,128]{2,1,0:T(8,128)(2,1)} %w_hbm.1, ...), custom_call_target="tpu_custom_call" | custom-call | tf_op jit(solution)/shard_map/pallas_call | solution.py:307
  29.4 1.8 %shard_map.104 = (f32[64,128]{1,0:T(8,128)}, f32[88,128]{1,0:T(8,128)}, f32[8,128]{1,0:T(8,128)}) custom-call(f32[64,128]{1,0:T(8,128)} %get-tuple-element.10.state_hbm, f32[8,128]{1,0:T(8,128)} %get-tuple-element.11.regrid_hbm, bf16[96,192]{1,0:T(8,128)(2,1)} %get-tuple-element.12.hot_hbm, f32[192,128]{1,0:T(8,128)} %bitcast.4, f32[88,128]{1,0:T(8,128)} %dep_hbm.3, ...), custom_call_target="tpu_custom_call" | custom-call | tf_op jit(solution)/shard_map/pallas_call | solution.py:332

commit v4 on v3

--- a/solution.py
+++ b/solution.py
@@ -53,7 +53,7 @@
 
     barrier = pltpu.get_barrier_semaphore()
     greet = [(f, lax.rem(t + k, TILES)) for k in FAR_FIRST]
-    greet += [(fa, ti) for fa in (up, down) for ti in (left, t, right)]
+    greet += [(fa, ti) for ti in (left, right, t) for fa in (up, down)]
     for device in greet:
         pl.semaphore_signal(barrier, inc=1, device_id=device, device_id_type=MESH)
 
@@ -92,13 +92,12 @@
     for copy in dest_copies:
         copy.start()
 
-    halo = [
-        (pack.at[pl.ds(0, 56)], rows_below, (up, t)),
-        (pack.at[pl.ds(24, 56)], rows_above, (down, t)),
-    ]
-    for face, slot in ((up, 2), (f, 1), (down, 0)):
+    halo = []
+    for face, slot in ((up, 2), (down, 0), (f, 1)):
         halo.append((strip_first, side.at[slot, pl.ds(0, 8)], (face, left)))
         halo.append((strip_last, side.at[slot, pl.ds(120, 8)], (face, right)))
+    halo.append((pack.at[pl.ds(0, 56)], rows_below, (up, t)))
+    halo.append((pack.at[pl.ds(24, 56)], rows_above, (down, t)))
     for i, (src, dst, device) in enumerate(halo):
         halo_copies.append(pltpu.make_async_remote_copy(
             src_ref=src, dst_ref=dst, send_sem=halo_send_sem.at[i], recv_sem=halo_recv_sem.at[i],
@@ -153,7 +152,7 @@
     blocks = jnp.concatenate([hi, lo, wet_v[...].astype(F32).astype(BF16)], 1)
     block_id = (lax.broadcasted_iota(jnp.int32, (TILES * SLOTS, CELLS), 1) + 1).astype(F32)
     for copy in dest_copies:
-        copy.wait()
+        copy.wait_recv()
     local = jnp.concatenate([dest_all[i] for i in range(TILES)], 0) - BLOCKS * t
     asked = slots_of(((local >= 0) & (local < BLOCKS)).astype(F32))
     local = (local + 1).astype(F32)
@@ -188,7 +187,7 @@
     first, last = lane == 0, lane == CELLS - 1
 
     for copy in halo_copies:
-        copy.wait()
+        copy.wait_recv()
     sides = [jnp.swapaxes(side[k], 0, 1) for k in range(3)]
     main = [rows_above[8 * i:8 * i + 8, :] for i in range(6)]
     main += [pack[8 + 8 * r:16 + 8 * r, :] for r in range(ROWS)]
@@ -253,7 +252,7 @@
     outs[2].start()
 
     for copy in sea_copies:
-        copy.wait()
+        copy.wait_recv()
     pieces = [sea_recv[i].astype(F32) for i in range(TILES)]
     parts = [jnp.concatenate([p[SLOTS * part:SLOTS * (part + 1)] for p in pieces], 0) for part in range(3)]
     got = jnp.dot(place_t[...], jnp.concatenate(parts, 1).astype(BF16), preferred_element_type=F32)
@@ -270,6 +269,8 @@
 
     for copy in outs + h_copies:
         copy.wait()
+    for copy in dest_copies + halo_copies + sea_copies:
+        copy.wait_send()
 
 
 def finish(

time: 31.5 us -> 31.3 us (level)
  no operation moved by 1% of the time
where the time goes in v4:
time: 31.3 us; the launch traced here: 31.1 us
  Pallas kernels  30.4 us (97%)
  between operations  0.64 us (2%)
    pallas_call x1, Pallas kernels, body(): pl.pallas_call(functools.partial(kernel, faces), out_shape=(state_shape,...  28.7 us
    pallas_call x1, Pallas kernels, body(): pl.pallas_call(finish, out_shape=(state_shape, sea_shape, regrid_shape),...  1.77 us

profile of v4, /device:TPU:1, one launch (start us, length us, event | category | flops | bytes accessed | tf_op | source)
XLA Modules:
  0.0 31.1 jit_solution(10036333353791470768)
XLA Ops:
  0.6 28.7 %shard_map.103 = (f32[64,128]{1,0:T(8,128)}, f32[8,128]{1,0:T(8,128)}, bf16[96,192]{1,0:T(8,128)(2,1)}, f32[8,24,128]{2,1,0:T(8,128)}) custom-call(f32[64,128]{1,0:T(8,128)} %bitcast.5, f32[8,128]{1,0:T(8,128)} %courant_hbm.1, f32[8,8]{1,0:T(8,128)} %proj_hbm.1, s32[1,88]{1,0:T(1,128)} %bitcast.6, bf16[88,128,128]{2,1,0:T(8,128)(2,1)} %w_hbm.1, ...), custom_call_target="tpu_custom_call" | custom-call | tf_op jit(solution)/shard_map/pallas_call | solution.py:308
  29.3 1.8 %shard_map.104 = (f32[64,128]{1,0:T(8,128)}, f32[88,128]{1,0:T(8,128)}, f32[8,128]{1,0:T(8,128)}) custom-call(f32[64,128]{1,0:T(8,128)} %get-tuple-element.10.state_hbm, f32[8,128]{1,0:T(8,128)} %get-tuple-element.11.regrid_hbm, bf16[96,192]{1,0:T(8,128)(2,1)} %get-tuple-element.12.hot_hbm, f32[192,128]{1,0:T(8,128)} %bitcast.4, f32[88,128]{1,0:T(8,128)} %dep_hbm.3, ...), custom_call_target="tpu_custom_call" | custom-call | tf_op jit(solution)/shard_map/pallas_call | solution.py:333
